TPU v7x, 128 devices: a whole 4x4x4 slice. The times are simulated.
128 devices in a mesh: expert: 16 (over z, y), tensor: 8 (over x, core).
Axes of the slice: x: 4, y: 4, z: 4, core: 2. Of those that a mesh axis runs over, the one named last changes fastest.
Arguments:
- tokens: bfloat16 [4096, 4096], P('expert'), may hold values from -6 to 6
- picked: int32 [8, 16, 32], P(None, 'expert'), may hold values from 0 to 255, as said below
- counts: int32 [8, 16], replicated, may hold values from 1 to 32, 256 in all within a row
- combine: float32 [8, 16, 32], P(None, 'expert'), may hold values from 0.1 to 1
- w_in: bfloat16 [16, 4096, 4096], P('expert', None, 'tensor'), may hold values from -0.09375 to 0.09375
- w_out: bfloat16 [16, 4096, 4096], P('expert', 'tensor'), may hold values from -0.09375 to 0.09375
- w_qkv: bfloat16 [4096, 32, 3, 128], P('tensor', 'expert'), may hold values from -0.09375 to 0.09375
- upstream: bfloat16 [4096, 4096], P('expert'), may hold values from -6 to 6
Outputs:
- projected: bfloat16 [4096, 32, 3, 128], P('tensor', 'expert')
- grad_tokens: bfloat16 [4096, 4096], P('expert', 'tensor')
- grad_in: bfloat16 [16, 4096, 4096], P('expert', None, 'tensor')
- grad_out: bfloat16 [16, 4096, 4096], P('expert', 'tensor')
Inputs may be any that keep to these rules, and one draw needn't show every extreme that they name: `picked`: only slots k < counts[e, s] are used; the used entries of one expert and one shard are distinct. Each expert's counts sum to 256; in every expert some shard gives exactly 32 rows.
All inputs are finite; a program needn't handle non-finite values.
Results may differ from a plain program's by a relative error of at most 0.02.
Values may be sent and summed in bfloat16 or wider, within the bound.
A program may use at most 128 MiB of HBM per device.

v0:
```python
import jax
import jax.numpy as jnp
from jax import lax
from jax.sharding import PartitionSpec as P


def gelu_value(value):
    return 0.5 * value * (1.0 + lax.erf(value * 0.7071067811865476))


def gelu_slope(value):
    return (
        0.5 * (1.0 + lax.erf(value * 0.7071067811865476))
        + value * jnp.exp(-0.5 * value * value) * 0.3989422804014327
    )


def on_device(tokens, picked, counts, combine, w_in, w_out, w_qkv, upstream):
    source_count = lax.axis_size("expert")
    tensor_count = lax.axis_size("tensor")
    source = lax.axis_index("expert")
    part = lax.axis_index("tensor")
    tok_dev, width = tokens.shape
    experts, capacity = (picked.shape[0], picked.shape[2])
    slice_w = width // tensor_count
    padded_rows = source_count * capacity
    contract_last = (((1,), (1,)), ((), ()))
    contract_first = (((0,), (0,)), ((), ()))
    picks = picked[:, 0, :]
    own_counts = lax.dynamic_slice_in_dim(counts, source, 1, 1)[:, 0]
    slot_ids = jnp.arange(capacity, dtype=jnp.int32)
    in_use = slot_ids[None, :] < own_counts[:, None]
    weights = jnp.where(in_use, combine[:, 0, :], 0.0)
    owner_table = (
        (picks[:, :, None] == jnp.arange(tok_dev, dtype=jnp.int32)[None, None, :])
        & in_use[:, :, None]
    ).astype(jnp.float32)

    def to_experts(chosen):
        doubled = jnp.repeat(chosen, 2, axis=0)
        arrived = lax.all_to_all(doubled, "expert", split_axis=0, concat_axis=0, tiled=True)
        return arrived.reshape(padded_rows, width)

    def reduce_rows(partial_value):
        return lax.psum_scatter(
            partial_value.astype(jnp.bfloat16), "tensor", scatter_dimension=1, tiled=True
        )

    def send_back(values):
        arrived = lax.all_to_all(
            values.reshape(source_count, capacity, slice_w),
            "expert",
            split_axis=0,
            concat_axis=0,
            tiled=True,
        )
        half_pairs = arrived.reshape(experts, 2, capacity, slice_w).astype(jnp.float32)
        return half_pairs[:, 0] + half_pairs[:, 1]

    chosen = jnp.where(in_use[:, :, None], tokens[picks], jnp.zeros((), jnp.bfloat16))
    expert_rows = to_experts(chosen)
    preact = jnp.dot(expert_rows, w_in[0], preferred_element_type=jnp.float32)
    hidden = gelu_value(preact).astype(jnp.bfloat16)
    partial_value = jnp.dot(hidden, w_out[0], preferred_element_type=jnp.float32)
    halves = send_back(reduce_rows(partial_value))
    mixture = jnp.einsum(
        "ect,ecd->td", owner_table, weights[:, :, None] * halves, precision=lax.Precision.HIGHEST
    )
    own_slice = lax.dynamic_slice_in_dim(tokens, part * slice_w, slice_w, 1)
    layer_output = (own_slice.astype(jnp.float32) + mixture).astype(jnp.bfloat16)
    flat_qkv = w_qkv.reshape(slice_w, -1)
    products = jnp.dot(
        lax.all_gather(layer_output, "expert", axis=0, tiled=True),
        flat_qkv,
        preferred_element_type=jnp.float32,
    )
    projected = lax.psum_scatter(
        products.astype(jnp.bfloat16), "tensor", scatter_dimension=0, tiled=True
    )
    projected = projected.reshape(-1, w_qkv.shape[1], w_qkv.shape[2], w_qkv.shape[3])
    scaled = jnp.where(
        in_use[:, :, None], weights[:, :, None] * upstream[picks].astype(jnp.float32), 0.0
    ).astype(jnp.bfloat16)
    row_grad = to_experts(scaled)
    hidden_grad = lax.dot_general(
        row_grad, w_out[0], contract_last, preferred_element_type=jnp.float32
    )
    preact_grad = (hidden_grad * gelu_slope(preact)).astype(jnp.bfloat16)
    grad_out = lax.dot_general(
        hidden, row_grad, contract_first, preferred_element_type=jnp.float32
    ).astype(jnp.bfloat16)[None]
    grad_in = lax.dot_general(
        expert_rows, preact_grad, contract_first, preferred_element_type=jnp.float32
    ).astype(jnp.bfloat16)[None]
    back_rows = lax.dot_general(
        preact_grad, w_in[0], contract_last, preferred_element_type=jnp.float32
    )
    returned = send_back(reduce_rows(back_rows))
    back_mixture = jnp.einsum("ect,ecd->td", owner_table, returned, precision=lax.Precision.HIGHEST)
    upstream_slice = lax.dynamic_slice_in_dim(upstream, part * slice_w, slice_w, 1)
    grad_tokens = (upstream_slice.astype(jnp.float32) + back_mixture).astype(jnp.bfloat16)
    return (projected, grad_tokens, grad_in, grad_out)


def solution(mesh):
    return jax.shard_map(
        on_device,
        mesh=mesh,
        in_specs=(
            P("expert", None),
            P(None, "expert", None),
            P(),
            P(None, "expert", None),
            P("expert", None, "tensor"),
            P("expert", "tensor", None),
            P("tensor", "expert", None, None),
            P("expert", None),
        ),
        out_specs=(
            P("tensor", "expert", None, None),
            P("expert", "tensor"),
            P("expert", None, "tensor"),
            P("expert", "tensor", None),
        ),
        check_vma=False,
    )
```

profile of v0, /device:TPU:5, one launch (start us, length us, event | category | flops | bytes accessed | tf_op | source)
XLA Modules:
  0.0 308.8 jit_solution(11386793657130481137)
XLA Ops:
  7.2 0.0 copy-start
  7.2 0.0 reduce-scatter.4.cloned.1.call-start
  7.2 0.7 compare_select_fusion
  7.9 0.1 reshape.128
  8.0 0.0 copy-done
  8.0 0.2 dynamic-slice_reduce_fusion
  8.2 0.1 iota_compare_fusion.1
  8.3 5.7 %gather_fusion = bf16[256,4096]{1,0:T(8,128)(2,1)S(1)} fusion(bf16[256,4096]{1,0:T(8,128)(2,1)} %param.8, s32[1024]{0:T(1024)S(1)} %pad_clamp_fusion), kind=kCustom, calls=%fused_computation | custom fusion | bytes 4195328 | tf_op jit(solution)/shard_map/gather | solution.py:60
  14.0 0.2 broadcast_select_fusion
  14.2 0.5 broadcast_in_dim.50
  14.8 0.0 copy-start.11
  14.8 57.7 %all_to_all.20 = bf16[16,32,4096]{2,1,0:T(8,128)(2,1)S(1)} all-to-all(bf16[16,32,4096]{2,1,0:T(8,128)(2,1)S(1)} %bitcast.68), channel_id=1, replica_groups=mesh['expert'=16,'tensor'=8] {'expert'}, dimensions={0} | all-to-all | bytes 8388608 | tf_op jit(solution)/shard_map/all_to_all | solution.py:41
  72.4 2.0 copy-done.4
  74.5 0.0 copy-done.11
  74.5 2.3 fusion.8
  76.8 0.0 copy-start.5
  76.8 1.0 copy-done.5
  77.8 0.0 copy-done.9
  77.8 4.4 %convolution_convert_fusion.4 = bf16[512,4096]{1,0:T(8,128)(2,1)} fusion(bf16[1,512,4096]{2,1,0:T(8,128)(2,1)S(1)} %copy-done.9, f32[512,512]{1,0:T(8,128)S(1)} %fusion.8), kind=kOutput, calls=%fused_computation.6 | convolution fusion | flops 2150891520 | bytes 9437184 | tf_op jit(solution)/shard_map/dot_general | solution.py:64
  82.2 0.0 reduce-scatter.4.cloned.1.call-update
  82.2 32.9 %reduce-scatter.4.cloned.1.call-done = bf16[512,512]{1,0:T(8,128)(2,1)} async-done(((bf16[512,4096]{1,0:T(8,128)(2,1)}), bf16[512,512]{1,0:T(8,128)(2,1)}) %reduce-scatter.4.cloned.1.call-update) | async-done | bytes 524304 | tf_op jit(solution)/shard_map/reduce_scatter | solution.py:45
  115.1 6.7 %all-to-all-start.1 = ((bf16[16,32,512]{2,1,0:T(8,128)(2,1)}), bf16[16,32,512]{2,1,0:T(8,128)(2,1)S(1)}, u32[]{:S(2)}, u32[]{:S(2)}) async-start(bf16[16,32,512]{2,1,0:T(8,128)(2,1)} %bitcast.79), calls=%async_computation.2 | async-start | bytes 1048576 | tf_op jit(solution)/shard_map/all_to_all | solution.py:50
  121.8 0.0 all-gather.2.cloned.1.call-start
  121.9 0.0 copy-done.7
  121.9 0.1 broadcast_select_fusion.1
  121.9 11.2 %all-to-all-done.1 = bf16[16,32,512]{2,1,0:T(8,128)(2,1)S(1)} async-done(((bf16[16,32,512]{2,1,0:T(8,128)(2,1)}), bf16[16,32,512]{2,1,0:T(8,128)(2,1)S(1)}, u32[]{:S(2)}, u32[]{:S(2)}) %all-to-all-start.1) | async-done | bytes 524320 | tf_op jit(solution)/shard_map/all_to_all | solution.py:50
  133.2 0.1 convert.2
  133.3 0.0 copy-done.8
  133.3 2.2 fusion.19
  135.5 0.0 all-gather.2.cloned.1.call-update
  135.6 0.0 reduce-scatter.8.cloned.1.call-start
  135.6 0.0 copy-done.2
  135.6 3.2 %gather_fusion.1 = bf16[256,4096]{1,0:T(8,128)(2,1)} fusion(bf16[256,4096]{1,0:T(8,128)(2,1)S(1)} %copy-done.2, s32[1024]{0:T(1024)S(1)} %pad_clamp_fusion), kind=kCustom, calls=%fused_computation.1 | custom fusion | bytes 4195328 | tf_op jit(solution)/shard_map/gather | solution.py:82
  138.8 2.4 fusion.3
  141.2 0.5 broadcast_in_dim.52
  141.7 0.0 copy-start.6
  141.7 0.0 copy-start.10
  141.7 58.8 %all_to_all.21 = bf16[16,32,4096]{2,1,0:T(8,128)(2,1)S(1)} all-to-all(bf16[16,32,4096]{2,1,0:T(8,128)(2,1)S(1)} %bitcast.69), channel_id=1, replica_groups=mesh['expert'=16,'tensor'=8] {'expert'}, dimensions={0} | all-to-all | bytes 8388608 | tf_op jit(solution)/shard_map/all_to_all | solution.py:41
  200.5 2.1 copy-done.3
  202.6 0.0 copy-done.6
  202.6 0.0 copy-done.10
  202.6 2.8 fusion.13
  205.4 0.0 copy-start.13
  205.4 0.8 copy-done.13
  206.2 0.0 copy-done.12
  206.2 4.5 %convolution_convert_fusion.3 = bf16[512,4096]{1,0:T(8,128)(2,1)} fusion(bf16[512,512]{1,0:T(8,128)(2,1)S(1)} %fusion.13, bf16[1,4096,512]{2,1,0:T(8,128)(2,1)S(1)} %copy-done.12), kind=kOutput, calls=%fused_computation.5 | convolution fusion | flops 2149580800 | bytes 8912896 | tf_op jit(solution)/shard_map/dot_general | solution.py:95
  210.7 0.0 reduce-scatter.8.cloned.1.call-update
  210.7 0.0 reduce-scatter.6.cloned.1.call-start
  210.7 3.0 copy.13
  213.8 2.8 all-gather.2.cloned.1.call-done
  216.6 8.5 %convolution_convert_fusion = bf16[4096,768]{1,0:T(8,128)(2,1)} fusion(bf16[4096,512]{1,0:T(8,128)(2,1)} %all-gather.2.cloned.1.call-done, bf16[512,768]{0,1:T(8,128)(2,1)} %bitcast.77), kind=kOutput, calls=%fused_computation.2 | convolution fusion | flops 3224371200 | bytes 11272192 | tf_op jit(solution)/shard_map/dot_general | solution.py:72
  225.1 0.0 reduce-scatter.6.cloned.1.call-update
  225.1 6.6 %fusion.1 = bf16[1,512,4096]{2,1,0:T(8,128)(2,1)} fusion(bf16[512,4096]{1,0:T(8,128)(2,1)} %bitcast.67, f32[512,512]{1,0:T(8,128)S(1)} %copy-done.6), kind=kOutput, calls=%fused_computation.8 | convolution fusion | flops 2150891520 | bytes 9437184 | tf_op jit(solution)/shard_map/dot_general | solution.py:89
  231.8 20.8 %reduce-scatter.8.cloned.1.call-done = bf16[512,512]{1,0:T(8,128)(2,1)} async-done(((bf16[512,4096]{1,0:T(8,128)(2,1)}), bf16[512,512]{1,0:T(8,128)(2,1)}) %reduce-scatter.8.cloned.1.call-update) | async-done | bytes 524304 | tf_op jit(solution)/shard_map/reduce_scatter | solution.py:45
  252.6 6.7 %all-to-all-start.3 = ((bf16[16,32,512]{2,1,0:T(8,128)(2,1)}), bf16[16,32,512]{2,1,0:T(8,128)(2,1)S(1)}, u32[]{:S(2)}, u32[]{:S(2)}) async-start(bf16[16,32,512]{2,1,0:T(8,128)(2,1)} %bitcast.78), calls=%async_computation.6 | async-start | bytes 1048576 | tf_op jit(solution)/shard_map/all_to_all | solution.py:50
  259.3 0.0 copy-start.1
  259.3 6.7 %fusion = bf16[1,4096,512]{2,1,0:T(8,128)(2,1)} fusion(bf16[512,4096]{1,0:T(8,128)(2,1)} %bitcast.73, bf16[512,512]{1,0:T(8,128)(2,1)} %copy-done.13), kind=kOutput, calls=%fused_computation.7 | convolution fusion | flops 2149580800 | bytes 8912896 | tf_op jit(solution)/shard_map/dot_general | solution.py:92
  266.0 4.6 %all-to-all-done.3 = bf16[16,32,512]{2,1,0:T(8,128)(2,1)S(1)} async-done(((bf16[16,32,512]{2,1,0:T(8,128)(2,1)}), bf16[16,32,512]{2,1,0:T(8,128)(2,1)S(1)}, u32[]{:S(2)}, u32[]{:S(2)}) %all-to-all-start.3) | async-done | bytes 524320 | tf_op jit(solution)/shard_map/all_to_all | solution.py:50
  270.7 0.1 convert.3
  270.8 1.3 fusion.18
  272.1 27.0 %reduce-scatter.6.cloned.1.call-done = bf16[512,768]{1,0:T(8,128)(2,1)} async-done(((bf16[4096,768]{1,0:T(8,128)(2,1)}), bf16[512,768]{1,0:T(8,128)(2,1)}) %reduce-scatter.6.cloned.1.call-update) | async-done | bytes 786448 | tf_op jit(solution)/shard_map/reduce_scatter | solution.py:77
  299.1 1.4 copy.14
  300.5 1.8 copy.15
  302.3 0.0 copy-done.1
  (8 shorter events, 0.0 us)
Async XLA Ops:
  7.2 0.9 copy-start
  7.2 107.9 %reduce-scatter.4.cloned.1.call-start = ((), (), s32[]{:S(2)}) async-start(), calls=%async_computation.7 | async-start | bytes 4718592 | tf_op jit(solution)/shard_map/reduce_scatter | solution.py:45
  14.8 59.7 %copy-start.11 = (bf16[1,4096,512]{2,1,0:T(8,128)(2,1)S(1)}, bf16[1,4096,512]{2,1,0:T(8,128)(2,1)}, u32[]{:S(2)}) copy-start(bf16[1,4096,512]{2,1,0:T(8,128)(2,1)} %param.12) | copy-start | bytes 12582916
  72.4 2.1 copy-start.4
  74.5 3.3 %copy-start.9 = (bf16[1,512,4096]{2,1,0:T(8,128)(2,1)S(1)}, bf16[1,512,4096]{2,1,0:T(8,128)(2,1)}, u32[]{:S(2)}) copy-start(bf16[1,512,4096]{2,1,0:T(8,128)(2,1)} %param.13) | copy-start | bytes 12582916
  76.8 1.0 copy-start.5
  82.2 39.7 %copy-start.7 = (f32[8,1,32]{2,1,0:T(1,128)S(1)}, f32[8,1,32]{2,1,0:T(1,128)}, u32[]{:S(2)}) copy-start(f32[8,1,32]{2,1,0:T(1,128)} %param.11) | copy-start | bytes 3076
  82.2 51.1 %copy-start.8 = (s32[8,1,32]{2,1,0:T(1,128)S(1)}, s32[8,1,32]{2,1,0:T(1,128)}, u32[]{:S(2)}) copy-start(s32[8,1,32]{2,1,0:T(1,128)} %param.9) | copy-start | bytes 3076
  82.2 53.4 %copy-start.2 = (bf16[256,4096]{1,0:T(8,128)(2,1)S(1)}, bf16[256,4096]{1,0:T(8,128)(2,1)}, u32[]{:S(2)}) copy-start(bf16[256,4096]{1,0:T(8,128)(2,1)} %param.15) | copy-start | bytes 6291460
  115.1 18.1 %all-to-all-start.1 = ((bf16[16,32,512]{2,1,0:T(8,128)(2,1)}), bf16[16,32,512]{2,1,0:T(8,128)(2,1)S(1)}, u32[]{:S(2)}, u32[]{:S(2)}) async-start(bf16[16,32,512]{2,1,0:T(8,128)(2,1)} %bitcast.79), calls=%async_computation.2 | async-start | bytes 1048576 | tf_op jit(solution)/shard_map/all_to_all | solution.py:50
  121.8 94.8 %all-gather.2.cloned.1.call-start = ((), (), s32[]{:S(2)}) async-start(), calls=%async_computation.8 | async-start | bytes 4456448 | tf_op jit(solution)/shard_map/all_gather | solution.py:73
  135.6 117.0 %reduce-scatter.8.cloned.1.call-start = ((), (), s32[]{:S(2)}) async-start(), calls=%async_computation.10 | async-start | bytes 4718592 | tf_op jit(solution)/shard_map/reduce_scatter | solution.py:45
  141.7 60.9 %copy-start.6 = (f32[512,512]{1,0:T(8,128)S(1)}, f32[512,512]{1,0:T(8,128)}, u32[]{:S(2)}) copy-start(f32[512,512]{1,0:T(8,128)} %copy-done.5) | copy-start | bytes 3145732
  141.7 60.9 %copy-start.10 = (bf16[1,512,4096]{2,1,0:T(8,128)(2,1)S(1)}, bf16[1,512,4096]{2,1,0:T(8,128)(2,1)}, u32[]{:S(2)}) copy-start(bf16[1,512,4096]{2,1,0:T(8,128)(2,1)} %param.13) | copy-start | bytes 12582916
  200.5 2.1 copy-start.3
  202.6 3.6 %copy-start.12 = (bf16[1,4096,512]{2,1,0:T(8,128)(2,1)S(1)}, bf16[1,4096,512]{2,1,0:T(8,128)(2,1)}, u32[]{:S(2)}) copy-start(bf16[1,4096,512]{2,1,0:T(8,128)(2,1)} %param.12) | copy-start | bytes 12582916
  205.4 0.8 copy-start.13
  210.7 88.4 %reduce-scatter.6.cloned.1.call-start = ((), (), s32[]{:S(2)}) async-start(), calls=%async_computation.9 | async-start | bytes 7077888 | tf_op jit(solution)/shard_map/reduce_scatter | solution.py:77
  252.6 18.1 %all-to-all-start.3 = ((bf16[16,32,512]{2,1,0:T(8,128)(2,1)}), bf16[16,32,512]{2,1,0:T(8,128)(2,1)S(1)}, u32[]{:S(2)}, u32[]{:S(2)}) async-start(bf16[16,32,512]{2,1,0:T(8,128)(2,1)} %bitcast.78), calls=%async_computation.6 | async-start | bytes 1048576 | tf_op jit(solution)/shard_map/all_to_all | solution.py:50
  259.3 43.0 %copy-start.1 = (s32[8,16]{1,0:T(8,128)S(1)}, s32[8,16]{1,0:T(8,128)}, u32[]{:S(2)}) copy-start(s32[8,16]{1,0:T(8,128)} %param.10) | copy-start | bytes 1540
Sparse Core Ops, SparseCore 0:
  82.3 32.6 reduce-scatter.3
  135.7 80.8 all-gather.1
  219.6 32.9 reduce-scatter.7
  254.8 44.2 reduce-scatter.5
where the time goes:
time: 311 us; the launch traced here: 309 us
  blocking collectives  116 us (37%)
  waiting for transfers between devices  99.4 us (32%)
  matrix products  39.4 us (13%)
  local copies, waits for them, and re-layouts  22.4 us (7%)
  between operations  14 us (5%)
  starting transfers between devices  13.7 us (4%)
  other arithmetic  3.69 us (1%)
    all_to_all x2, blocking collectives, to_experts(): lax.all_to_all(doubled, 'expert', split_axis=0, concat_axis=0, tiled=True)  116 us
    reduce_scatter x2, waiting for transfers between devices, reduce_rows(): lax.psum_scatter(partial_value.astype(jnp.bfloat16), 'tensor', scatter_di...  53.7 us
    reduce_scatter x1, waiting for transfers between devices, on_device(): lax.psum_scatter(products.astype(jnp.bfloat16), 'tensor', scatter_dimensi...  27 us
    all_to_all x2, waiting for transfers between devices, send_back(): lax.all_to_all(values.reshape(source_count, capacity, slice_w), 'expert',...  15.8 us
    all_to_all x2, starting transfers between devices, send_back(): lax.all_to_all(values.reshape(source_count, capacity, slice_w), 'expert',...  13.5 us
    unnamed x30, local copies, waits for them, and re-layouts  10.8 us
    dot_general x1, matrix products, on_device(): jnp.dot(lax.all_gather(layer_output, 'expert', axis=0, tiled=True), flat_...  8.52 us
    dot_general x1, matrix products, on_device(): lax.dot_general(expert_rows, preact_grad, contract_first, preferred_eleme...  6.71 us
  transfers between devices with their start and end apart: 6, of which 6 were waited for; matrix products, arithmetic and copies ran while one was open for 13% of the time, Pallas kernels for 0%

commit v1 on v0

v1 whole, which is shorter than its diff:
```python
import jax
import jax.numpy as jnp
from jax import lax
from jax.experimental import pallas as pl
from jax.experimental.pallas import tpu as pltpu
from jax.sharding import PartitionSpec as P

BF = jnp.bfloat16
F32 = jnp.float32
NN = (((1,), (0,)), ((), ()))
NT = (((1,), (1,)), ((), ()))
TN = (((0,), (0,)), ((), ()))
RING = 4


def dot(a, b, dims=NN):
    return lax.dot_general(a, b, dims, preferred_element_type=F32)


class Wires:
    def __init__(self, send_sems, recv_sems):
        self.send_sems, self.recv_sems = send_sems, recv_sems
        self.next = 0
        self.sent = []

    def take(self, count=1):
        first = self.next
        self.next += count
        return first

    def copy(self, slot, src, dst, device):
        return pltpu.make_async_remote_copy(
            src_ref=src,
            dst_ref=dst,
            send_sem=self.send_sems.at[slot],
            recv_sem=self.recv_sems.at[slot],
            device_id=device,
            device_id_type=pl.DeviceIdType.MESH,
        )

    def send(self, slot, src, dst, device, keep=True):
        copy = self.copy(slot, src, dst, device)
        copy.start()
        if keep:
            self.sent.append(copy)

    def arrived(self, slot, dst, device):
        self.copy(slot, dst, dst, device).wait_recv()


class RingGather:
    def __init__(self, wires, at, me, minus, plus, far, to_minus, to_plus):
        self.w, self.at = wires, at
        self.me, self.minus, self.plus, self.far = me, minus, plus, far
        self.to_minus, self.to_plus = to_minus, to_plus
        self.base = wires.take(6)

    def start(self):
        b = self.base
        for i, half in enumerate((1, 0)):
            ref = self.at(self.me, half)
            self.w.send(b + i, ref, ref, self.to_plus)
            ref = self.at(self.me, 1 - half)
            self.w.send(b + 3 + i, ref, ref, self.to_minus)

    def forward(self):
        b = self.base
        ref = self.at(self.minus, 1)
        self.w.arrived(b, ref, self.to_plus)
        self.w.send(b + 2, ref, ref, self.to_plus)
        ref = self.at(self.plus, 0)
        self.w.arrived(b + 3, ref, self.to_minus)
        self.w.send(b + 5, ref, ref, self.to_minus)

    def near(self):
        self.w.arrived(self.base + 1, self.at(self.minus, 0), self.to_plus)
        self.w.arrived(self.base + 4, self.at(self.plus, 1), self.to_minus)

    def last(self):
        self.w.arrived(self.base + 2, self.at(self.far, 1), self.to_plus)
        self.w.arrived(self.base + 5, self.at(self.far, 0), self.to_minus)


def layer_kernel(
    tokens, upstream, w_in, w_out, w_qkv, picked, counts, combine,
    projected, grad_tokens, rows_out, rgrad_out, hidden_out, pgrad_out,
    tok, ups, win, wout, sel, comp, wcol,
    send_f, send_b, recv_f, recv_b, ag_f, ag_b,
    acc, slope, hid, pgr,
    pst, d2d, sbuf, half_l, half_r, full_l, full_r,
    ret_s, ret_r, lay, stage, d2dp, hl, hr, fl, fr,
    load_sems, send_sems, recv_sems,
):
    s, t = lax.axis_index("expert"), lax.axis_index("tensor")
    z, y = s // RING, s % RING
    x, c = t // 2, t % 2
    shards, experts, cap = 16, counts.shape[0], combine.shape[1]
    n_tok, width = tok.shape
    half_rows = n_tok // 2
    quarter = n_tok // 4

    def wrap(v):
        return lax.rem(v + RING, RING)

    left, right = wrap(x - 1) * 2 + c, wrap(x + 1) * 2 + c
    far = wrap(x + 2) * 2 + c
    sib = x * 2 + 1 - c
    to_left, to_right, to_sib = (s, left), (s, right), (s, sib)
    y_minus, y_plus, y_far = wrap(y - 1), wrap(y + 1), wrap(y + 2)
    z_minus, z_plus, z_far = wrap(z - 1), wrap(z + 1), wrap(z + 2)
    to_ym, to_yp = (z * RING + y_minus, t), (z * RING + y_plus, t)
    to_zm, to_zp = (z_minus * RING + y, t), (z_plus * RING + y, t)

    cols = pl.ds(pl.multiple_of(t * width, width), width)
    load_tok = pltpu.make_async_copy(tokens.at[:, cols], tok, load_sems.at[0])
    load_ups = pltpu.make_async_copy(upstream.at[:, cols], ups, load_sems.at[1])
    load_win = pltpu.make_async_copy(w_in.at[0], win, load_sems.at[2])
    load_wout = pltpu.make_async_copy(w_out.at[0], wout, load_sems.at[3])
    load_tok.start()
    load_ups.start()
    load_win.start()
    load_wout.start()

    barrier = pltpu.get_barrier_semaphore()

    def greet(i, carry):
        pl.semaphore_signal(
            barrier, inc=1, device_id=(lax.rem(s + i, shards), t),
            device_id_type=pl.DeviceIdType.MESH,
        )
        return carry

    lax.fori_loop(1, shards, greet, 0)
    for device in (to_left, to_right, to_sib):
        pl.semaphore_signal(
            barrier, inc=1, device_id=device, device_id_type=pl.DeviceIdType.MESH
        )

    slots = experts * cap
    lane = lax.broadcasted_iota(jnp.int32, (1, slots), 1)
    spread = (
        lax.broadcasted_iota(jnp.int32, (cap, slots), 1) % cap
        == lax.broadcasted_iota(jnp.int32, (cap, slots), 0)
    )
    spread = jnp.where(spread, 1.0, 0.0).astype(BF)
    wide = dot(picked[...].astype(F32).astype(BF), spread)
    own_row = (
        lax.broadcasted_iota(jnp.int32, (experts, slots), 1) // cap
        == lax.broadcasted_iota(jnp.int32, (experts, slots), 0)
    )
    pick_row = jnp.sum(jnp.where(own_row, wide, 0.0), axis=0, keepdims=True).astype(jnp.int32)
    count_row = jnp.zeros((1, slots), jnp.int32)
    for e in range(experts):
        count_row = jnp.where(lane // cap == e, counts[e, s], count_row)
    pick_row = jnp.where(lane % cap < count_row, pick_row, -1)
    token_ids = lax.broadcasted_iota(jnp.int32, (n_tok, slots), 0)
    sel[...] = jnp.where(token_ids == pick_row, 1.0, 0.0).astype(BF)

    eye = (
        lax.broadcasted_iota(jnp.int32, (cap, cap), 0)
        == lax.broadcasted_iota(jnp.int32, (cap, cap), 1)
    )
    turned = lax.dot_general(
        jnp.where(eye, 1.0, 0.0).astype(F32), combine[...], NT,
        precision=lax.Precision.HIGHEST, preferred_element_type=F32,
    )
    for e in range(experts):
        wcol[e * cap:(e + 1) * cap, :] = turned[:, e:e + 1]

    load_tok.wait()
    send_f[...] = dot(sel[...], tok[...], TN).astype(BF).reshape(send_f.shape)

    padded = shards * cap
    lane = lax.broadcasted_iota(jnp.int32, (1, padded), 1)
    mine = s // 2
    offset = jnp.int32(0)
    offset_row = jnp.zeros((1, padded), jnp.int32)
    count_row = jnp.zeros((1, padded), jnp.int32)
    for shard in range(shards):
        count = counts[mine, shard]
        here = lane // cap == shard
        offset_row = jnp.where(here, offset, offset_row)
        count_row = jnp.where(here, count, count_row)
        offset = offset + count
    position = jnp.where(lane % cap < count_row, offset_row + lane % cap, -1)
    row_ids = lax.broadcasted_iota(jnp.int32, comp.shape, 0)
    comp[...] = jnp.where(row_ids == position, 1.0, 0.0).astype(BF)

    pl.semaphore_wait(barrier, shards - 1 + 3)

    w = Wires(send_sems, recv_sems)

    def exchange(src_at, recv):
        base = w.take(shards)

        def body(i, carry):
            to = lax.rem(s + i, shards)
            w.send(base + i, src_at(to), recv.at[s], (to, t), keep=False)
            return carry

        lax.fori_loop(1, shards, body, 0)
        recv[s] = src_at(s)[...]
        return base

    def exchanged(base, recv):
        def body(i, carry):
            source = lax.rem(s - i + shards, shards)
            w.arrived(base + i, recv.at[source], (source, t))
            return carry

        lax.fori_loop(1, shards, body, 0)

    def exchange_end(base, recv):
        def body(i, carry):
            w.copy(base + i, recv.at[0], recv.at[0], to_sib).wait_send()
            return carry

        lax.fori_loop(1, shards, body, 0)

    ex_f = exchange(lambda to: send_f.at[to // 2], recv_f)

    load_ups.wait()
    taken = dot(sel[...], ups[...], TN)
    send_b[...] = (taken * wcol[...]).astype(BF).reshape(send_b.shape)
    ex_b = exchange(lambda to: send_b.at[to // 2], recv_b)

    class RowGather:
        def __init__(self, buf):
            self.buf = buf

            def at(block, half):
                return buf.at[block, pl.ds(half * half_rows, half_rows), :]

            self.ring = RingGather(w, at, t, left, right, far, to_left, to_right)
            self.base = w.take(7)
            self.at = at

        def give(self, k, ref):
            w.send(self.base + k, ref, ref, to_sib)

        def start(self):
            self.ring.start()
            self.give(0, self.buf.at[t])

        def forward(self):
            self.ring.forward()
            self.give(1, self.at(left, 1))
            self.give(2, self.at(right, 0))

        def near(self):
            self.ring.near()
            self.give(3, self.at(left, 0))
            self.give(4, self.at(right, 1))

        def last(self):
            self.ring.last()
            self.give(5, self.at(far, 1))
            self.give(6, self.at(far, 0))

        def sib_own(self):
            w.arrived(self.base, self.buf.at[sib], to_sib)

        def sib_near(self):
            other = 1 - 2 * c
            for k, (block, half) in enumerate(((left, 1), (right, 0), (left, 0), (right, 1))):
                w.arrived(self.base + 1 + k, self.at(block + other, half), to_sib)

        def sib_last(self):
            other = 1 - 2 * c
            w.arrived(self.base + 5, self.at(far + other, 1), to_sib)
            w.arrived(self.base + 6, self.at(far + other, 0), to_sib)

    other = 1 - 2 * c

    def win_at(j):
        return win[pl.ds(pl.multiple_of(j * width, width), width), :]

    def wout_at(j):
        return wout[:, pl.ds(pl.multiple_of(j * width, width), width)]

    def gathered(gather, weight_at, dims):
        buf = gather.buf

        def add(j, first=False):
            term = dot(buf[j], weight_at(j), dims)
            if first:
                acc[...] = term
            else:
                acc[...] += term

        add(t, True)
        gather.sib_own()
        add(sib)
        gather.near()
        add(left)
        add(right)
        gather.last()
        gather.sib_near()
        add(left + other)
        add(right + other)
        add(far)
        gather.sib_last()
        add(far + other)

    class RowReduce:
        def __init__(self, k):
            self.k = k
            self.base = w.take(10)

        def partials(self, lhs, weight_at, dims):
            k, b = self.k, self.base
            for d in (2, 1, 3, 0):
                j = wrap(x + d) * 2 + 1 - c
                pst[k, d] = dot(lhs[...], weight_at(j), dims).astype(BF)
                w.send(b + d, pst.at[k, d], d2d.at[k, d], to_sib)
            lo, hi = pl.ds(0, half_rows), pl.ds(half_rows, half_rows)
            for d in (2, 1, 3, 0):
                j = wrap(x + d) * 2 + c
                own = dot(lhs[...], weight_at(j), dims)
                w.arrived(b + d, d2d.at[k, d], to_sib)
                sbuf[k, d] = (own + d2d[k, d].astype(F32)).astype(BF)
                if d == 2:
                    w.send(b + 4, sbuf.at[k, d, hi], half_l.at[k], to_right)
                    w.send(b + 5, sbuf.at[k, d, lo], half_r.at[k], to_left)
                elif d == 1:
                    w.send(b + 6, sbuf.at[k, d, lo], full_l.at[k, lo], to_right)
                elif d == 3:
                    w.send(b + 7, sbuf.at[k, d, hi], full_r.at[k, hi], to_left)

        def forward(self):
            k, b = self.k, self.base
            lo, hi = pl.ds(0, half_rows), pl.ds(half_rows, half_rows)
            w.arrived(b + 4, half_l.at[k], to_right)
            sbuf[k, 1, hi] = (sbuf[k, 1, hi].astype(F32) + half_l[k].astype(F32)).astype(BF)
            w.send(b + 8, sbuf.at[k, 1, hi], full_l.at[k, hi], to_right)
            w.arrived(b + 5, half_r.at[k], to_left)
            sbuf[k, 3, lo] = (sbuf[k, 3, lo].astype(F32) + half_r[k].astype(F32)).astype(BF)
            w.send(b + 9, sbuf.at[k, 3, lo], full_r.at[k, lo], to_left)

        def result(self):
            k, b = self.k, self.base
            lo, hi = pl.ds(0, half_rows), pl.ds(half_rows, half_rows)
            w.arrived(b + 6, full_l.at[k, lo], to_right)
            w.arrived(b + 7, full_r.at[k, hi], to_left)
            w.arrived(b + 8, full_l.at[k, hi], to_right)
            w.arrived(b + 9, full_r.at[k, lo], to_left)
            total = sbuf[k, 0].astype(F32) + full_l[k].astype(F32) + full_r[k].astype(F32)
            return total.astype(BF)

    def send_back(k, rows):
        ret_s[k] = dot(comp[...], rows, TN).astype(BF).reshape(ret_s.shape[1:])
        return exchange(lambda to: ret_s.at[k, to], ret_r.at[k])

    def returned(k, base):
        exchanged(base, ret_r.at[k])
        pairs = ret_r[k].reshape(experts, 2, cap, width).astype(F32)
        return (pairs[:, 0] + pairs[:, 1]).reshape(slots, width)

    def scatter(values):
        high = values.astype(BF)
        low = (values - high.astype(F32)).astype(BF)
        return dot(sel[...], high) + dot(sel[...], low)

    gather_f = RowGather(ag_f)
    gather_b = RowGather(ag_b)
    exchanged(ex_f, recv_f)
    ag_f[t] = dot(comp[...], recv_f[...].reshape(padded, width)).astype(BF)
    gather_f.start()
    gather_f.forward()
    load_win.wait()
    gathered(gather_f, win_at, NN)
    pre = acc[...]
    cdf = 0.5 * (1.0 + lax.erf(pre * 0.7071067811865476))
    hid[...] = (pre * cdf).astype(BF)
    slope[...] = cdf + pre * jnp.exp(-0.5 * pre * pre) * 0.3989422804014327
    load_wout.wait()
    reduce_f = RowReduce(0)
    reduce_f.partials(hid, wout_at, NN)

    save_rows = pltpu.make_async_copy(ag_f, rows_out, load_sems.at[0])
    save_rows.start()
    save_hid = pltpu.make_async_copy(hid, hidden_out, load_sems.at[1])
    save_hid.start()

    exchanged(ex_b, recv_b)
    ag_b[t] = dot(comp[...], recv_b[...].reshape(padded, width)).astype(BF)
    reduce_f.forward()
    gather_b.start()
    back_f = send_back(0, reduce_f.result())
    gather_b.forward()

    halves = returned(0, back_f)
    mixture = scatter(halves * wcol[...])
    lay[s] = (tok[...].astype(F32) + mixture).astype(BF)

    def lay_at(part, along_z, fixed):
        def at(pos, half):
            index = pos * RING + fixed if along_z else fixed + pos
            return lay.at[index, pl.ds(part * half_rows + half * quarter, quarter), :]
        return at

    def along_y(part, zz):
        return RingGather(
            w, lay_at(part, False, zz * RING), y, y_minus, y_plus, y_far, to_ym, to_yp
        )

    def along_z(part, yy):
        return RingGather(
            w, lay_at(part, True, yy), z, z_minus, z_plus, z_far, to_zm, to_zp
        )

    first_p, first_q = along_y(0, z), along_z(1, y)
    second_p = [along_z(0, yy) for yy in (y, y_minus, y_plus, y_far)]
    second_q = [along_y(1, zz) for zz in (z, z_minus, z_plus, z_far)]
    first_p.start()
    first_q.start()
    second_p[0].start()
    second_q[0].start()

    first_p.forward()
    first_q.forward()
    gathered(gather_b, wout_at, NT)
    pgr[...] = (acc[...] * slope[...]).astype(BF)
    save_rgrad = pltpu.make_async_copy(ag_b, rgrad_out, load_sems.at[2])
    save_rgrad.start()
    save_pgr = pltpu.make_async_copy(pgr, pgrad_out, load_sems.at[3])
    save_pgr.start()

    first_p.near()
    first_q.near()
    for k in (1, 2):
        second_p[k].start()
        second_q[k].start()
    first_p.last()
    first_q.last()
    second_p[3].start()
    second_q[3].start()
    second_p[0].forward()
    second_q[0].forward()

    reduce_b = RowReduce(1)
    reduce_b.partials(pgr, win_at, NT)

    for k in (1, 2):
        second_p[k].forward()
        second_q[k].forward()

    unit_base = w.take(8)
    x_base = w.take(12)

    def unit(q, zp, cp):
        for i in range(2):
            block = lay[zp * RING + cp * 2 + i, q * half_rows:(q + 1) * half_rows, :]
            stage[q, cp, zp, i * half_rows:(i + 1) * half_rows, :] = dot(
                block, w_qkv[...]
            ).astype(BF)

        @pl.when(cp != c)
        def _():
            w.send(
                unit_base + q * RING + zp, stage.at[q, cp, zp], d2dp.at[q, zp], to_sib,
                keep=False,
            )

    lo, hi = pl.ds(0, half_rows), pl.ds(half_rows, half_rows)

    def settle(q, zp):
        b = x_base + q * 6
        w.arrived(unit_base + q * RING + zp, d2dp.at[q, zp], to_sib)
        stage[q, c, zp] = (
            stage[q, c, zp].astype(F32) + d2dp[q, zp].astype(F32)
        ).astype(BF)
        d = wrap(zp - x)

        @pl.when(d == 2)
        def _():
            w.send(b, stage.at[q, c, zp, hi], hl.at[q], to_right, keep=False)
            w.send(b + 1, stage.at[q, c, zp, lo], hr.at[q], to_left, keep=False)

        @pl.when(d == 1)
        def _():
            w.send(b + 2, stage.at[q, c, zp, lo], fl.at[q, lo], to_right, keep=False)

        @pl.when(d == 3)
        def _():
            w.send(b + 3, stage.at[q, c, zp, hi], fr.at[q, hi], to_left, keep=False)

    def pass_on(q):
        b = x_base + q * 6
        zr, zl = wrap(x + 1), wrap(x - 1)
        w.arrived(b, hl.at[q], to_right)
        stage[q, c, zr, hi] = (
            stage[q, c, zr, hi].astype(F32) + hl[q].astype(F32)
        ).astype(BF)
        w.send(b + 4, stage.at[q, c, zr, hi], fl.at[q, hi], to_right, keep=False)
        w.arrived(b + 1, hr.at[q], to_left)
        stage[q, c, zl, lo] = (
            stage[q, c, zl, lo].astype(F32) + hr[q].astype(F32)
        ).astype(BF)
        w.send(b + 5, stage.at[q, c, zl, lo], fr.at[q, lo], to_left, keep=False)

    def finish(q):
        b = x_base + q * 6
        w.arrived(b + 2, fl.at[q, lo], to_right)
        w.arrived(b + 3, fr.at[q, hi], to_left)
        w.arrived(b + 4, fl.at[q, hi], to_right)
        w.arrived(b + 5, fr.at[q, lo], to_left)
        total = (
            stage[q, c, x].astype(F32) + fl[q].astype(F32) + fr[q].astype(F32)
        ).astype(BF)
        for i in range(2):
            first = i * n_tok + q * half_rows
            projected[first:first + half_rows, :] = total[i * half_rows:(i + 1) * half_rows]

    z_order = (z, z_plus, z_minus, z_far)
    pair = y // 2

    unit(0, z, 0)
    unit(0, z, 1)
    reduce_b.forward()
    for k in range(4):
        second_q[k].near()
    second_p[3].forward()
    second_q[3].forward()
    for zp in z_order:
        unit(1, zp, pair)
    settle(0, z)
    back_b = send_back(1, reduce_b.result())
    for k in range(4):
        second_p[k].near()
    for zp in (z_plus, z_minus):
        unit(0, zp, 0)
        unit(0, zp, 1)

    @pl.when(pair == c)
    def _():
        for zp in z_order:
            settle(1, zp)

    for k in range(4):
        second_p[k].last()
    unit(0, z_far, 0)
    unit(0, z_far, 1)
    for zp in (z_plus, z_minus, z_far):
        settle(0, zp)
    for k in range(4):
        second_q[k].last()
    for zp in z_order:
        unit(1, zp, 1 - pair)
    pass_on(0)

    @pl.when(pair != c)
    def _():
        for zp in z_order:
            settle(1, zp)

    back_rows = scatter(returned(1, back_b))
    grad_tokens[...] = (ups[...].astype(F32) + back_rows).astype(BF)
    pass_on(1)
    finish(0)
    finish(1)

    for copy in w.sent:
        copy.wait_send()
    exchange_end(ex_f, recv_f)
    exchange_end(ex_b, recv_b)
    exchange_end(back_f, ret_r.at[0])
    exchange_end(back_b, ret_r.at[1])

    for q in range(2):
        for k in range(RING):
            w.copy(unit_base + q * RING + k, d2dp.at[q, k], d2dp.at[q, k], to_sib).wait_send()
        for k in range(6):
            w.copy(x_base + q * 6 + k, hl.at[q], hl.at[q], to_left).wait_send()
    save_rows.wait()
    save_hid.wait()
    save_rgrad.wait()
    save_pgr.wait()


def weight_grad_kernel(rows, rgrad, hidden, pgrad, grad_in, grad_out):
    grad_in[0] = dot(rows[0], pgrad[...], TN).astype(BF)
    grad_out[0] = dot(hidden[...], rgrad[0], TN).astype(BF)


def on_device(tokens, picked, counts, combine, w_in, w_out, w_qkv, upstream):
    n_tok, width = tokens.shape
    experts, cap = picked.shape[0], picked.shape[2]
    parts, shards = 8, 16
    slice_w = width // parts
    rows = experts * cap
    hidden = w_in.shape[2]
    flat = w_qkv.reshape(slice_w, -1)
    columns = flat.shape[1]
    half = n_tok // 2
    anywhere = pl.BlockSpec(memory_space=pl.ANY)
    vmem = pl.BlockSpec(memory_space=pltpu.VMEM)
    smem = pl.BlockSpec(memory_space=pltpu.SMEM)
    sems = 340
    out = pl.pallas_call(
        layer_kernel,
        out_shape=(
            jax.ShapeDtypeStruct((2 * n_tok, columns), BF),
            jax.ShapeDtypeStruct((n_tok, slice_w), BF),
            jax.ShapeDtypeStruct((parts, rows, slice_w), BF),
            jax.ShapeDtypeStruct((parts, rows, slice_w), BF),
            jax.ShapeDtypeStruct((rows, hidden), BF),
            jax.ShapeDtypeStruct((rows, hidden), BF),
        ),
        in_specs=[anywhere] * 4 + [vmem, vmem, smem, vmem],
        out_specs=[vmem, vmem] + [anywhere] * 4,
        scratch_shapes=[
            pltpu.VMEM((n_tok, slice_w), BF),
            pltpu.VMEM((n_tok, slice_w), BF),
            pltpu.VMEM((width, hidden), BF),
            pltpu.VMEM((hidden, width), BF),
            pltpu.VMEM((n_tok, rows), BF),
            pltpu.VMEM((rows, shards * cap), BF),
            pltpu.VMEM((rows, 1), F32),
            pltpu.VMEM((experts, cap, slice_w), BF),
            pltpu.VMEM((experts, cap, slice_w), BF),
            pltpu.VMEM((shards, cap, slice_w), BF),
            pltpu.VMEM((shards, cap, slice_w), BF),
            pltpu.VMEM((parts, rows, slice_w), BF),
            pltpu.VMEM((parts, rows, slice_w), BF),
            pltpu.VMEM((rows, hidden), F32),
            pltpu.VMEM((rows, hidden), F32),
            pltpu.VMEM((rows, hidden), BF),
            pltpu.VMEM((rows, hidden), BF),
            pltpu.VMEM((2, RING, rows, slice_w), BF),
            pltpu.VMEM((2, RING, rows, slice_w), BF),
            pltpu.VMEM((2, RING, rows, slice_w), BF),
            pltpu.VMEM((2, rows // 2, slice_w), BF),
            pltpu.VMEM((2, rows // 2, slice_w), BF),
            pltpu.VMEM((2, rows, slice_w), BF),
            pltpu.VMEM((2, rows, slice_w), BF),
            pltpu.VMEM((2, shards, cap, slice_w), BF),
            pltpu.VMEM((2, shards, cap, slice_w), BF),
            pltpu.VMEM((shards, n_tok, slice_w), BF),
            pltpu.VMEM((2, 2, RING, n_tok, columns), BF),
            pltpu.VMEM((2, RING, n_tok, columns), BF),
            pltpu.VMEM((2, half, columns), BF),
            pltpu.VMEM((2, half, columns), BF),
            pltpu.VMEM((2, n_tok, columns), BF),
            pltpu.VMEM((2, n_tok, columns), BF),
            pltpu.SemaphoreType.DMA((4,)),
            pltpu.SemaphoreType.DMA((sems,)),
            pltpu.SemaphoreType.DMA((sems,)),
        ],
        compiler_params=pltpu.CompilerParams(
            collective_id=0, has_side_effects=True, vmem_limit_bytes=62 * 1024 * 1024
        ),
        cost_estimate=pl.CostEstimate(
            flops=8 * 10**9, bytes_accessed=20 * 10**6, transcendentals=3 * 10**5
        ),
        name="moe_layer",
    )(
        tokens, upstream, w_in, w_out, flat,
        picked[:, 0, :], counts, combine[:, 0, :],
    )
    projected, grad_tokens, taken, row_grad, hid, preact_grad = out
    whole = lambda shape: pl.BlockSpec(shape, lambda j: (0, 0))
    grad_in, grad_out = pl.pallas_call(
        weight_grad_kernel,
        grid=(parts,),
        out_shape=(
            jax.ShapeDtypeStruct(w_in.shape, BF),
            jax.ShapeDtypeStruct(w_out.shape, BF),
        ),
        in_specs=[
            pl.BlockSpec((1, rows, slice_w), lambda j: (j, 0, 0)),
            pl.BlockSpec((1, rows, slice_w), lambda j: (j, 0, 0)),
            whole((rows, hidden)),
            whole((rows, hidden)),
        ],
        out_specs=(
            pl.BlockSpec((1, slice_w, hidden), lambda j: (0, j, 0)),
            pl.BlockSpec((1, hidden, slice_w), lambda j: (0, 0, j)),
        ),
        compiler_params=pltpu.CompilerParams(vmem_limit_bytes=32 * 1024 * 1024),
        cost_estimate=pl.CostEstimate(
            flops=2 * 10**9, bytes_accessed=12 * 10**6, transcendentals=0
        ),
        name="weight_grads",
    )(taken, row_grad, hid, preact_grad)
    return (projected.reshape(2 * n_tok, *w_qkv.shape[1:]), grad_tokens, grad_in, grad_out)


def solution(mesh):
    return jax.shard_map(
        on_device,
        mesh=mesh,
        in_specs=(
            P("expert", None),
            P(None, "expert", None),
            P(),
            P(None, "expert", None),
            P("expert", None, "tensor"),
            P("expert", "tensor", None),
            P("tensor", "expert", None, None),
            P("expert", None),
        ),
        out_specs=(
            P("tensor", "expert", None, None),
            P("expert", "tensor"),
            P("expert", None, "tensor"),
            P("expert", "tensor", None),
        ),
        check_vma=False,
    )
```

time: 311 us -> 134 us (0.43)
  Pallas kernels: 0 us -> 120 us
  blocking collectives: 116 us -> 0 us
  waiting for transfers between devices: 99.4 us -> 0 us
  matrix products: 39.4 us -> 0 us
  starting transfers between devices: 13.7 us -> 0 us
  between operations: 14 us -> 0.66 us
  local copies, waits for them, and re-layouts: 22.4 us -> 12.4 us
  other arithmetic: 3.69 us -> 0 us
    pallas_call x0 -> x2, Pallas kernels: none -> 120 us  [the longest x1 114 us: on_device(): pl.pallas_call(layer_kernel, out_shape=(jax.ShapeDtypeStruct((2 * n_tok,...]
    all_to_all x2 -> x0, blocking collectives: 116 us -> none  [to_experts(): lax.all_to_all(doubled, 'expert', split_axis=0, concat_axis=0, tiled=True)]
    reduce_scatter x3 -> x0, waiting for transfers between devices: 80.7 us -> none  [the longest x2 53.7 us: reduce_rows(): lax.psum_scatter(partial_value.astype(jnp.bfloat16), 'tensor', scatter_di...]
    dot_general x9 -> x0, matrix products: 39.4 us -> none  [the longest x1 8.52 us: on_device(): jnp.dot(lax.all_gather(layer_output, 'expert', axis=0, tiled=True), flat_...]
    all_to_all x2 -> x0, waiting for transfers between devices: 15.8 us -> none  [send_back(): lax.all_to_all(values.reshape(source_count, capacity, slice_w), 'expert',...]
    all_to_all x2 -> x0, starting transfers between devices: 13.5 us -> none  [send_back(): lax.all_to_all(values.reshape(source_count, capacity, slice_w), 'expert',...]
    gather x2 -> x0, local copies, waits for them, and re-layouts: 8.92 us -> none  [the longest x1 5.75 us: on_device(): tokens[picks]]
    unnamed x30 -> x13, local copies, waits for them, and re-layouts: 10.8 us -> 9.84 us
  transfers between devices with their start and end apart: 6 -> 0, of which waited for: 6 -> 0; matrix products, arithmetic and copies ran while one was open for 13% -> 0% of each run, Pallas kernels for 0% -> 0%
where the time goes in v1:
time: 134 us; the launch traced here: 133 us
  Pallas kernels  120 us (90%)
  local copies, waits for them, and re-layouts  12.4 us (9%)
    pallas_call x1, Pallas kernels, on_device(): pl.pallas_call(layer_kernel, out_shape=(jax.ShapeDtypeStruct((2 * n_tok,...  114 us
    unnamed x13, local copies, waits for them, and re-layouts  9.84 us
    pallas_call x1, Pallas kernels, on_device(): pl.pallas_call(weight_grad_kernel, grid=(parts,), out_shape=(jax.ShapeDty...  5.66 us

profile of v1, /device:TPU:5, one launch (start us, length us, event | category | flops | bytes accessed | tf_op | source)
XLA Modules:
  0.0 133.1 jit_solution(11221155037366956060)
XLA Ops:
  0.6 2.3 %copy.14 = bf16[512,2,3,128]{0,3,2,1:T(8,128)(2,1)S(1)} copy(bf16[512,2,3,128]{3,1,2,0:T(2,128)(2,1)} %param.14) | data formatting | bytes 1572864 | tf_op args[6]
  2.9 1.2 copy.15.w_qkv
  4.0 114.3 %moe_layer.1 = (bf16[512,768]{1,0:T(8,128)(2,1)}, bf16[256,512]{1,0:T(8,128)(2,1)}, bf16[8,256,512]{2,1,0:T(8,128)(2,1)}, bf16[8,256,512]{2,1,0:T(8,128)(2,1)}, ...) custom-call(bf16[256,4096]{1,0:T(8,128)(2,1)} %tokens.1, bf16[256,4096]{1,0:T(8,128)(2,1)} %upstream.1, ...), custom_call_target="tpu_custom_call" | custom-call | flops 8000000000 | bytes 20000000 | tf_op jit(solution)/shard_map/moe_layer/pallas_call | solution.py:600
  118.4 1.4 %copy.16 = bf16[512,768]{0,1:T(8,128)(2,1)S(1)} copy(bf16[512,768]{1,0:T(8,128)(2,1)} %get-tuple-element.12) | data formatting | bytes 1572864 | tf_op jit(solution)/shard_map/moe_layer/pallas_call | solution.py:600
  119.8 0.0 copy-start.4
  119.8 1.8 %copy.17 = bf16[512,2,3,128]{3,1,2,0:T(2,128)(2,1)} copy(bf16[512,2,3,128]{0,3,2,1:T(8,128)(2,1)S(1)} %bitcast.4) | data formatting | bytes 1572864
  121.6 0.0 copy-start
  121.6 1.6 %copy-done = bf16[8,256,512]{2,1,0:T(8,128)(2,1)S(1)} copy-done((bf16[8,256,512]{2,1,0:T(8,128)(2,1)S(1)}, bf16[8,256,512]{2,1,0:T(8,128)(2,1)}, u32[]{:S(2)}) %copy-start) | copy-done | bytes 2097176
  123.2 0.0 copy-start.1
  123.2 1.6 %copy-done.1 = bf16[8,256,512]{2,1,0:T(8,128)(2,1)S(1)} copy-done((bf16[8,256,512]{2,1,0:T(8,128)(2,1)S(1)}, bf16[8,256,512]{2,1,0:T(8,128)(2,1)}, u32[]{:S(2)}) %copy-start.1) | copy-done | bytes 2097176
  124.8 0.0 copy-start.2
  124.8 0.9 copy-done.2
  125.7 0.0 copy-start.3
  125.7 0.9 copy-done.3
  126.7 5.7 %weight_grads.1 = (bf16[1,4096,512]{2,1,0:T(8,128)(2,1)}, bf16[1,512,4096]{2,1,0:T(8,128)(2,1)}) custom-call(bf16[8,256,512]{2,1,0:T(8,128)(2,1)S(1)} %copy-done, bf16[8,256,512]{2,1,0:T(8,128)(2,1)S(1)} %copy-done.1, bf16[256,512]{1,0:T(8,128)(2,1)S(1)} %copy-done.2, bf16[256,512]{1,0:T(8,128)(2,1)S(1)} %copy-done.3), custom_call_target="tpu_custom_call" | custom-call | flops 2000000000 | bytes 12000000 | tf_op jit(solution)/shard_map/weight_grads/pallas_call | solution.py:663
  132.3 0.0 copy-done.4
  132.3 0.7 copy.19
Async XLA Ops:
  119.8 12.6 %copy-start.4 = (bf16[256,512]{1,0:T(8,128)(2,1)S(1)}, bf16[256,512]{1,0:T(8,128)(2,1)}, u32[]{:S(2)}) copy-start(bf16[256,512]{1,0:T(8,128)(2,1)} %get-tuple-element.33) | copy-start | bytes 786436
  121.6 1.6 %copy-start = (bf16[8,256,512]{2,1,0:T(8,128)(2,1)S(1)}, bf16[8,256,512]{2,1,0:T(8,128)(2,1)}, u32[]{:S(2)}) copy-start(bf16[8,256,512]{2,1,0:T(8,128)(2,1)} %get-tuple-element.14.rows) | copy-start | bytes 6291460
  123.2 1.6 %copy-start.1 = (bf16[8,256,512]{2,1,0:T(8,128)(2,1)S(1)}, bf16[8,256,512]{2,1,0:T(8,128)(2,1)}, u32[]{:S(2)}) copy-start(bf16[8,256,512]{2,1,0:T(8,128)(2,1)} %get-tuple-element.15.rgrad) | copy-start | bytes 6291460
  124.8 0.9 copy-start.2
  125.7 0.9 copy-start.3

commit v2 on v1

--- a/solution.py
+++ b/solution.py
@@ -11,10 +11,20 @@
 NT = (((1,), (1,)), ((), ()))
 TN = (((0,), (0,)), ((), ()))
 RING = 4
+BAND = 32
 
 
 def dot(a, b, dims=NN):
     return lax.dot_general(a, b, dims, preferred_element_type=F32)
+
+
+def row_permutation(blocks, gather):
+    n = BAND * blocks
+    a = lax.broadcasted_iota(jnp.int32, (n, n), 0)
+    b = lax.broadcasted_iota(jnp.int32, (n, n), 1)
+    if not gather:
+        a, b = b, a
+    return jnp.where((a % BAND) * blocks + a // BAND == b, 1.0, 0.0).astype(BF)
 
 
 class Wires:
@@ -84,7 +94,7 @@
 def layer_kernel(
     tokens, upstream, w_in, w_out, w_qkv, picked, counts, combine,
     projected, grad_tokens, rows_out, rgrad_out, hidden_out, pgrad_out,
-    tok, ups, win, wout, sel, comp, wcol,
+    tok, ups, ups_half, win, wout, wraw, wqkv, sel, comp, wcol,
     send_f, send_b, recv_f, recv_b, ag_f, ag_b,
     acc, slope, hid, pgr,
     pst, d2d, sbuf, half_l, half_r, full_l, full_r,
@@ -116,10 +126,15 @@
     load_ups = pltpu.make_async_copy(upstream.at[:, cols], ups, load_sems.at[1])
     load_win = pltpu.make_async_copy(w_in.at[0], win, load_sems.at[2])
     load_wout = pltpu.make_async_copy(w_out.at[0], wout, load_sems.at[3])
+    wide_cols = pl.ds(pl.multiple_of(c * RING * width, width), RING * width)
+    load_half = pltpu.make_async_copy(upstream.at[:, wide_cols], ups_half, load_sems.at[4])
+    load_qkv = pltpu.make_async_copy(w_qkv, wraw, load_sems.at[5])
     load_tok.start()
-    load_ups.start()
+    load_half.start()
     load_win.start()
     load_wout.start()
+    load_qkv.start()
+    load_ups.start()
 
     barrier = pltpu.get_barrier_semaphore()
 
@@ -156,6 +171,42 @@
     token_ids = lax.broadcasted_iota(jnp.int32, (n_tok, slots), 0)
     sel[...] = jnp.where(token_ids == pick_row, 1.0, 0.0).astype(BF)
 
+    load_tok.wait()
+    send_f[...] = dot(sel[...], tok[...], TN).astype(BF).reshape(send_f.shape)
+
+    pl.semaphore_wait(barrier, shards - 1 + 3)
+
+    w = Wires(send_sems, recv_sems)
+
+    def exchange(src_at, recv):
+        base = w.take(shards)
+
+        def body(i, carry):
+            to = lax.rem(s + i, shards)
+            w.send(base + i, src_at(to), recv.at[s], (to, t), keep=False)
+            return carry
+
+        lax.fori_loop(1, shards, body, 0)
+        recv[s] = src_at(s)[...]
+        return base
+
+    def exchanged(base, recv):
+        def body(i, carry):
+            source = lax.rem(s - i + shards, shards)
+            w.arrived(base + i, recv.at[source], (source, t))
+            return carry
+
+        lax.fori_loop(1, shards, body, 0)
+
+    def exchange_end(base, recv):
+        def body(i, carry):
+            w.copy(base + i, recv.at[0], recv.at[0], to_sib).wait_send()
+            return carry
+
+        lax.fori_loop(1, shards, body, 0)
+
+    ex_f = exchange(lambda to: send_f.at[to // 2], recv_f)
+
     eye = (
         lax.broadcasted_iota(jnp.int32, (cap, cap), 0)
         == lax.broadcasted_iota(jnp.int32, (cap, cap), 1)
@@ -166,9 +217,6 @@
     )
     for e in range(experts):
         wcol[e * cap:(e + 1) * cap, :] = turned[:, e:e + 1]
-
-    load_tok.wait()
-    send_f[...] = dot(sel[...], tok[...], TN).astype(BF).reshape(send_f.shape)
 
     padded = shards * cap
     lane = lax.broadcasted_iota(jnp.int32, (1, padded), 1)
@@ -186,43 +234,19 @@
     row_ids = lax.broadcasted_iota(jnp.int32, comp.shape, 0)
     comp[...] = jnp.where(row_ids == position, 1.0, 0.0).astype(BF)
 
-    pl.semaphore_wait(barrier, shards - 1 + 3)
-
-    w = Wires(send_sems, recv_sems)
-
-    def exchange(src_at, recv):
-        base = w.take(shards)
-
-        def body(i, carry):
-            to = lax.rem(s + i, shards)
-            w.send(base + i, src_at(to), recv.at[s], (to, t), keep=False)
-            return carry
-
-        lax.fori_loop(1, shards, body, 0)
-        recv[s] = src_at(s)[...]
-        return base
-
-    def exchanged(base, recv):
-        def body(i, carry):
-            source = lax.rem(s - i + shards, shards)
-            w.arrived(base + i, recv.at[source], (source, t))
-            return carry
-
-        lax.fori_loop(1, shards, body, 0)
-
-    def exchange_end(base, recv):
-        def body(i, carry):
-            w.copy(base + i, recv.at[0], recv.at[0], to_sib).wait_send()
-            return carry
-
-        lax.fori_loop(1, shards, body, 0)
-
-    ex_f = exchange(lambda to: send_f.at[to // 2], recv_f)
-
-    load_ups.wait()
-    taken = dot(sel[...], ups[...], TN)
-    send_b[...] = (taken * wcol[...]).astype(BF).reshape(send_b.shape)
-    ex_b = exchange(lambda to: send_b.at[to // 2], recv_b)
+    load_half.wait()
+    for k in range(RING):
+        part = slice(k * width, (k + 1) * width)
+        taken = dot(sel[...], ups_half[:, part], TN) * wcol[...]
+        send_b[:, :, part] = taken.astype(BF).reshape(experts, cap, width)
+
+    load_qkv.wait()
+    blocks = wqkv.shape[1] // 128
+    turn = row_permutation(blocks, True)
+    for f in range(0, width, BAND):
+        moved = dot(turn, wraw[f * blocks:(f + BAND) * blocks, :]).astype(BF)
+        for k in range(blocks):
+            wqkv[f:f + BAND, k * 128:(k + 1) * 128] = moved[k * BAND:(k + 1) * BAND]
 
     class RowGather:
         def __init__(self, buf):
@@ -362,10 +386,10 @@
         return dot(sel[...], high) + dot(sel[...], low)
 
     gather_f = RowGather(ag_f)
-    gather_b = RowGather(ag_b)
     exchanged(ex_f, recv_f)
     ag_f[t] = dot(comp[...], recv_f[...].reshape(padded, width)).astype(BF)
     gather_f.start()
+    ex_b = exchange(lambda to: send_b.at[to // 2], recv_b)
     gather_f.forward()
     load_win.wait()
     gathered(gather_f, win_at, NN)
@@ -377,17 +401,37 @@
     reduce_f = RowReduce(0)
     reduce_f.partials(hid, wout_at, NN)
 
-    save_rows = pltpu.make_async_copy(ag_f, rows_out, load_sems.at[0])
+    save_rows = pltpu.make_async_copy(ag_f, rows_out, load_sems.at[6])
     save_rows.start()
-    save_hid = pltpu.make_async_copy(hid, hidden_out, load_sems.at[1])
+    save_hid = pltpu.make_async_copy(hid, hidden_out, load_sems.at[7])
     save_hid.start()
 
+    reduce_f.forward()
+    back_f = send_back(0, reduce_f.result())
+
+    give_b = w.take(RING)
     exchanged(ex_b, recv_b)
-    ag_b[t] = dot(comp[...], recv_b[...].reshape(padded, width)).astype(BF)
-    reduce_f.forward()
-    gather_b.start()
-    back_f = send_back(0, reduce_f.result())
-    gather_b.forward()
+    for k in range(RING):
+        part = recv_b[:, :, k * width:(k + 1) * width].reshape(padded, width)
+        mine_k = ag_b.at[c * RING + k]
+        mine_k[...] = dot(comp[...], part).astype(BF)
+        w.send(give_b + k, mine_k, mine_k, to_sib)
+    for k in range(2 * RING):
+        j = c * RING + k if k < RING else (1 - c) * RING + k - RING
+        if k >= RING:
+            w.arrived(give_b + k - RING, ag_b.at[j], to_sib)
+        term = dot(ag_b[j], wout_at(j), NT)
+        if k == 0:
+            acc[...] = term
+        else:
+            acc[...] += term
+    pgr[...] = (acc[...] * slope[...]).astype(BF)
+    save_rgrad = pltpu.make_async_copy(ag_b, rgrad_out, load_sems.at[8])
+    save_rgrad.start()
+    save_pgr = pltpu.make_async_copy(pgr, pgrad_out, load_sems.at[9])
+    save_pgr.start()
+    reduce_b = RowReduce(1)
+    reduce_b.partials(pgr, win_at, NT)
 
     halves = returned(0, back_f)
     mixture = scatter(halves * wcol[...])
@@ -417,34 +461,6 @@
     second_p[0].start()
     second_q[0].start()
 
-    first_p.forward()
-    first_q.forward()
-    gathered(gather_b, wout_at, NT)
-    pgr[...] = (acc[...] * slope[...]).astype(BF)
-    save_rgrad = pltpu.make_async_copy(ag_b, rgrad_out, load_sems.at[2])
-    save_rgrad.start()
-    save_pgr = pltpu.make_async_copy(pgr, pgrad_out, load_sems.at[3])
-    save_pgr.start()
-
-    first_p.near()
-    first_q.near()
-    for k in (1, 2):
-        second_p[k].start()
-        second_q[k].start()
-    first_p.last()
-    first_q.last()
-    second_p[3].start()
-    second_q[3].start()
-    second_p[0].forward()
-    second_q[0].forward()
-
-    reduce_b = RowReduce(1)
-    reduce_b.partials(pgr, win_at, NT)
-
-    for k in (1, 2):
-        second_p[k].forward()
-        second_q[k].forward()
-
     unit_base = w.take(8)
     x_base = w.take(12)
 
@@ -452,7 +468,7 @@
         for i in range(2):
             block = lay[zp * RING + cp * 2 + i, q * half_rows:(q + 1) * half_rows, :]
             stage[q, cp, zp, i * half_rows:(i + 1) * half_rows, :] = dot(
-                block, w_qkv[...]
+                block, wqkv[...]
             ).astype(BF)
 
         @pl.when(cp != c)
@@ -515,17 +531,42 @@
     z_order = (z, z_plus, z_minus, z_far)
     pair = y // 2
 
-    unit(0, z, 0)
-    unit(0, z, 1)
+    first_p.forward()
+    first_q.forward()
+    second_p[0].forward()
+    second_q[0].forward()
+    first_p.near()
+    first_q.near()
+    for k in (1, 2):
+        second_p[k].start()
+        second_q[k].start()
     reduce_b.forward()
-    for k in range(4):
+    second_q[0].near()
+    unit(0, z, pair)
+    unit(1, z, pair)
+    first_p.last()
+    first_q.last()
+    second_p[3].start()
+    second_q[3].start()
+    unit(0, z, 1 - pair)
+    for k in (1, 2):
+        second_p[k].forward()
+        second_q[k].forward()
+    settle(0, z)
+
+    @pl.when(pair == c)
+    def _():
+        settle(1, z)
+
+    back_b = send_back(1, reduce_b.result())
+    for k in (1, 2):
         second_q[k].near()
+    unit(1, z_plus, pair)
+    unit(1, z_minus, pair)
     second_p[3].forward()
     second_q[3].forward()
-    for zp in z_order:
-        unit(1, zp, pair)
-    settle(0, z)
-    back_b = send_back(1, reduce_b.result())
+    second_q[3].near()
+    unit(1, z_far, pair)
     for k in range(4):
         second_p[k].near()
     for zp in (z_plus, z_minus):
@@ -534,19 +575,25 @@
 
     @pl.when(pair == c)
     def _():
-        for zp in z_order:
+        for zp in (z_plus, z_minus, z_far):
             settle(1, zp)
 
+    for zp in (z_plus, z_minus):
+        settle(0, zp)
     for k in range(4):
         second_p[k].last()
     unit(0, z_far, 0)
     unit(0, z_far, 1)
-    for zp in (z_plus, z_minus, z_far):
-        settle(0, zp)
     for k in range(4):
         second_q[k].last()
     for zp in z_order:
         unit(1, zp, 1 - pair)
+    settle(0, z_far)
+
+    @pl.when(pair == c)
+    def _():
+        pass_on(1)
+
     pass_on(0)
 
     @pl.when(pair != c)
@@ -554,9 +601,14 @@
         for zp in z_order:
             settle(1, zp)
 
+    load_ups.wait()
     back_rows = scatter(returned(1, back_b))
     grad_tokens[...] = (ups[...].astype(F32) + back_rows).astype(BF)
-    pass_on(1)
+
+    @pl.when(pair != c)
+    def _():
+        pass_on(1)
+
     finish(0)
     finish(1)
 
@@ -578,9 +630,20 @@
     save_pgr.wait()
 
 
-def weight_grad_kernel(rows, rgrad, hidden, pgrad, grad_in, grad_out):
+def weight_grad_kernel(
+    rows, rgrad, hidden, pgrad, products, grads, grad_in, grad_out, projected, grad_tokens
+):
     grad_in[0] = dot(rows[0], pgrad[...], TN).astype(BF)
     grad_out[0] = dot(hidden[...], rgrad[0], TN).astype(BF)
+    grad_tokens[...] = grads[...]
+    blocks = products.shape[1] // 128
+    turn = row_permutation(blocks, False)
+    for f in range(0, products.shape[0], BAND):
+        block = products[f:f + BAND, :]
+        stacked = jnp.concatenate(
+            [block[:, k * 128:(k + 1) * 128] for k in range(blocks)], axis=0
+        )
+        projected[f * blocks:(f + BAND) * blocks, :] = dot(turn, stacked).astype(BF)
 
 
 def on_device(tokens, picked, counts, combine, w_in, w_out, w_qkv, upstream):
@@ -590,8 +653,9 @@
     slice_w = width // parts
     rows = experts * cap
     hidden = w_in.shape[2]
-    flat = w_qkv.reshape(slice_w, -1)
-    columns = flat.shape[1]
+    heads, kinds, lanes = w_qkv.shape[1:]
+    columns = heads * kinds * lanes
+    flat = w_qkv.transpose(0, 2, 1, 3).reshape(slice_w * kinds * heads, lanes)
     half = n_tok // 2
     anywhere = pl.BlockSpec(memory_space=pl.ANY)
     vmem = pl.BlockSpec(memory_space=pltpu.VMEM)
@@ -607,20 +671,23 @@
             jax.ShapeDtypeStruct((rows, hidden), BF),
             jax.ShapeDtypeStruct((rows, hidden), BF),
         ),
-        in_specs=[anywhere] * 4 + [vmem, vmem, smem, vmem],
+        in_specs=[anywhere] * 5 + [vmem, smem, vmem],
         out_specs=[vmem, vmem] + [anywhere] * 4,
         scratch_shapes=[
             pltpu.VMEM((n_tok, slice_w), BF),
             pltpu.VMEM((n_tok, slice_w), BF),
+            pltpu.VMEM((n_tok, width // 2), BF),
             pltpu.VMEM((width, hidden), BF),
             pltpu.VMEM((hidden, width), BF),
+            pltpu.VMEM(flat.shape, BF),
+            pltpu.VMEM((slice_w, columns), BF),
             pltpu.VMEM((n_tok, rows), BF),
             pltpu.VMEM((rows, shards * cap), BF),
             pltpu.VMEM((rows, 1), F32),
             pltpu.VMEM((experts, cap, slice_w), BF),
-            pltpu.VMEM((experts, cap, slice_w), BF),
+            pltpu.VMEM((experts, cap, width // 2), BF),
             pltpu.VMEM((shards, cap, slice_w), BF),
-            pltpu.VMEM((shards, cap, slice_w), BF),
+            pltpu.VMEM((shards, cap, width // 2), BF),
             pltpu.VMEM((parts, rows, slice_w), BF),
             pltpu.VMEM((parts, rows, slice_w), BF),
             pltpu.VMEM((rows, hidden), F32),
@@ -643,7 +710,7 @@
             pltpu.VMEM((2, half, columns), BF),
             pltpu.VMEM((2, n_tok, columns), BF),
             pltpu.VMEM((2, n_tok, columns), BF),
-            pltpu.SemaphoreType.DMA((4,)),
+            pltpu.SemaphoreType.DMA((10,)),
             pltpu.SemaphoreType.DMA((sems,)),
             pltpu.SemaphoreType.DMA((sems,)),
         ],
@@ -658,32 +725,41 @@
         tokens, upstream, w_in, w_out, flat,
         picked[:, 0, :], counts, combine[:, 0, :],
     )
-    projected, grad_tokens, taken, row_grad, hid, preact_grad = out
+    products, grads, taken, row_grad, hid, preact_grad = out
     whole = lambda shape: pl.BlockSpec(shape, lambda j: (0, 0))
-    grad_in, grad_out = pl.pallas_call(
+    slab = lambda *shape: pl.BlockSpec(shape, lambda j: (j, 0))
+    step, grad_step = 2 * n_tok // parts, n_tok // parts
+    grad_in, grad_out, projected, grad_tokens = pl.pallas_call(
         weight_grad_kernel,
         grid=(parts,),
         out_shape=(
             jax.ShapeDtypeStruct(w_in.shape, BF),
             jax.ShapeDtypeStruct(w_out.shape, BF),
+            jax.ShapeDtypeStruct((2 * n_tok * kinds * heads, lanes), BF),
+            jax.ShapeDtypeStruct((n_tok, slice_w), BF),
         ),
         in_specs=[
             pl.BlockSpec((1, rows, slice_w), lambda j: (j, 0, 0)),
             pl.BlockSpec((1, rows, slice_w), lambda j: (j, 0, 0)),
             whole((rows, hidden)),
             whole((rows, hidden)),
+            slab(step, columns),
+            slab(grad_step, slice_w),
         ],
         out_specs=(
             pl.BlockSpec((1, slice_w, hidden), lambda j: (0, j, 0)),
             pl.BlockSpec((1, hidden, slice_w), lambda j: (0, 0, j)),
+            slab(step * kinds * heads, lanes),
+            slab(grad_step, slice_w),
         ),
-        compiler_params=pltpu.CompilerParams(vmem_limit_bytes=32 * 1024 * 1024),
+        compiler_params=pltpu.CompilerParams(vmem_limit_bytes=60 * 1024 * 1024),
         cost_estimate=pl.CostEstimate(
-            flops=2 * 10**9, bytes_accessed=12 * 10**6, transcendentals=0
+            flops=2 * 10**9, bytes_accessed=15 * 10**6, transcendentals=0
         ),
         name="weight_grads",
-    )(taken, row_grad, hid, preact_grad)
-    return (projected.reshape(2 * n_tok, *w_qkv.shape[1:]), grad_tokens, grad_in, grad_out)
+    )(taken, row_grad, hid, preact_grad, products, grads)
+    projected = projected.reshape(2 * n_tok, kinds, heads, lanes).transpose(0, 2, 1, 3)
+    return projected, grad_tokens, grad_in, grad_out
 
 
 def solution(mesh):

time: 134 us -> 124 us (0.925)
  local copies, waits for them, and re-layouts: 12.4 us -> 0 us
  Pallas kernels: 120 us -> 123 us
    unnamed x13 -> x0, local copies, waits for them, and re-layouts: 9.84 us -> none
    pallas_call x1, Pallas kernels: 5.66 us -> 9.04 us  [on_device(): pl.pallas_call(weight_grad_kernel, grid=(parts,), out_shape=(jax.ShapeDty...]
    pallas_call x1 -> x0, local copies, waits for them, and re-layouts: 1.41 us -> none  [on_device(): pl.pallas_call(layer_kernel, out_shape=(jax.ShapeDtypeStruct((2 * n_tok,...]
where the time goes in v2:
time: 124 us
  Pallas kernels  123 us (99%)
    pallas_call x1, Pallas kernels, on_device(): pl.pallas_call(layer_kernel, out_shape=(jax.ShapeDtypeStruct((2 * n_tok,...  114 us
    pallas_call x1, Pallas kernels, on_device(): pl.pallas_call(weight_grad_kernel, grid=(parts,), out_shape=(jax.ShapeDty...  9.04 us

profile of v2, /device:TPU:5, one launch (start us, length us, event | category | flops | bytes accessed | tf_op | source)
XLA Modules:
  0.0 124.0 jit_solution(12085011708748514865)
XLA Ops:
  0.6 114.2 %moe_layer.1 = (bf16[512,768]{1,0:T(8,128)(2,1)}, bf16[256,512]{1,0:T(8,128)(2,1)}, bf16[8,256,512]{2,1,0:T(8,128)(2,1)}, bf16[8,256,512]{2,1,0:T(8,128)(2,1)}, ...) custom-call(bf16[256,4096]{1,0:T(8,128)(2,1)} %tokens.1, bf16[256,4096]{1,0:T(8,128)(2,1)} %upstream.1, ...), custom_call_target="tpu_custom_call" | custom-call | flops 8000000000 | bytes 20000000 | tf_op jit(solution)/shard_map/moe_layer/pallas_call | solution.py:664
  114.8 9.0 %weight_grads.1 = (bf16[1,4096,512]{2,1,0:T(8,128)(2,1)}, bf16[1,512,4096]{2,1,0:T(8,128)(2,1)}, bf16[3072,128]{1,0:T(8,128)(2,1)}, bf16[256,512]{1,0:T(8,128)(2,1)}) custom-call(bf16[8,256,512]{2,1,0:T(8,128)(2,1)} %get-tuple-element.14.rows, bf16[8,256,512]{2,1,0:T(8,128)(2,1)} %get-tuple-element.15.rgrad, bf16[256,512]{1,0:T(8,128)(2,1)} %get-tuple-element.16.hidden, ...), custom_call_target="tpu_custom_call" | custom-call | flops 2000000000 | bytes 15000000 | tf_op jit(solution)/shard_map/weight_grads/pallas_call | solution.py:732

commit v3 on v2

--- a/solution.py
+++ b/solution.py
@@ -93,7 +93,7 @@
 
 def layer_kernel(
     tokens, upstream, w_in, w_out, w_qkv, picked, counts, combine,
-    projected, grad_tokens, rows_out, rgrad_out, hidden_out, pgrad_out,
+    projected, grad_tokens, grad_in, grad_out,
     tok, ups, ups_half, win, wout, wraw, wqkv, sel, comp, wcol,
     send_f, send_b, recv_f, recv_b, ag_f, ag_b,
     acc, slope, hid, pgr,
@@ -401,10 +401,6 @@
     reduce_f = RowReduce(0)
     reduce_f.partials(hid, wout_at, NN)
 
-    save_rows = pltpu.make_async_copy(ag_f, rows_out, load_sems.at[6])
-    save_rows.start()
-    save_hid = pltpu.make_async_copy(hid, hidden_out, load_sems.at[7])
-    save_hid.start()
 
     reduce_f.forward()
     back_f = send_back(0, reduce_f.result())
@@ -426,13 +422,6 @@
         else:
             acc[...] += term
     pgr[...] = (acc[...] * slope[...]).astype(BF)
-    save_rgrad = pltpu.make_async_copy(ag_b, rgrad_out, load_sems.at[8])
-    save_rgrad.start()
-    save_pgr = pltpu.make_async_copy(pgr, pgrad_out, load_sems.at[9])
-    save_pgr.start()
-    reduce_b = RowReduce(1)
-    reduce_b.partials(pgr, win_at, NT)
-
     halves = returned(0, back_f)
     mixture = scatter(halves * wcol[...])
     lay[s] = (tok[...].astype(F32) + mixture).astype(BF)
@@ -460,6 +449,9 @@
     first_q.start()
     second_p[0].start()
     second_q[0].start()
+
+    reduce_b = RowReduce(1)
+    reduce_b.partials(pgr, win_at, NT)
 
     unit_base = w.take(8)
     x_base = w.take(12)
@@ -540,7 +532,6 @@
     for k in (1, 2):
         second_p[k].start()
         second_q[k].start()
-    reduce_b.forward()
     second_q[0].near()
     unit(0, z, pair)
     unit(1, z, pair)
@@ -552,21 +543,29 @@
     for k in (1, 2):
         second_p[k].forward()
         second_q[k].forward()
+    reduce_b.forward()
     settle(0, z)
 
     @pl.when(pair == c)
     def _():
         settle(1, z)
 
-    back_b = send_back(1, reduce_b.result())
+    for j in range(2 * RING):
+        part = slice(j * width, (j + 1) * width)
+        grad_in[part, :] = dot(ag_f[j], pgr[...], TN).astype(BF)
     for k in (1, 2):
         second_q[k].near()
     unit(1, z_plus, pair)
     unit(1, z_minus, pair)
     second_p[3].forward()
     second_q[3].forward()
+    back_b = send_back(1, reduce_b.result())
     second_q[3].near()
     unit(1, z_far, pair)
+    hid_turned = hid[...].T
+    for j in range(2 * RING):
+        part = slice(j * width, (j + 1) * width)
+        grad_out[:, part] = dot(hid_turned, ag_b[j]).astype(BF)
     for k in range(4):
         second_p[k].near()
     for zp in (z_plus, z_minus):
@@ -624,18 +623,15 @@
             w.copy(unit_base + q * RING + k, d2dp.at[q, k], d2dp.at[q, k], to_sib).wait_send()
         for k in range(6):
             w.copy(x_base + q * 6 + k, hl.at[q], hl.at[q], to_left).wait_send()
-    save_rows.wait()
-    save_hid.wait()
-    save_rgrad.wait()
-    save_pgr.wait()
-
-
-def weight_grad_kernel(
-    rows, rgrad, hidden, pgrad, products, grads, grad_in, grad_out, projected, grad_tokens
+
+
+def write_kernel(
+    grad_in_v, grad_out_v, products, grads, projected, grad_tokens, grad_in, grad_out, sems
 ):
-    grad_in[0] = dot(rows[0], pgrad[...], TN).astype(BF)
-    grad_out[0] = dot(hidden[...], rgrad[0], TN).astype(BF)
-    grad_tokens[...] = grads[...]
+    copies = []
+    for src, dst in ((grad_in_v, grad_in.at[0]), (grad_out_v, grad_out.at[0]), (grads, grad_tokens)):
+        copies.append(pltpu.make_async_copy(src, dst, sems.at[len(copies)]))
+        copies[-1].start()
     blocks = products.shape[1] // 128
     turn = row_permutation(blocks, False)
     for f in range(0, products.shape[0], BAND):
@@ -644,6 +640,8 @@
             [block[:, k * 128:(k + 1) * 128] for k in range(blocks)], axis=0
         )
         projected[f * blocks:(f + BAND) * blocks, :] = dot(turn, stacked).astype(BF)
+    for copy in copies:
+        copy.wait()
 
 
 def on_device(tokens, picked, counts, combine, w_in, w_out, w_qkv, upstream):
@@ -664,15 +662,13 @@
     out = pl.pallas_call(
         layer_kernel,
         out_shape=(
-            jax.ShapeDtypeStruct((2 * n_tok, columns), BF),
-            jax.ShapeDtypeStruct((n_tok, slice_w), BF),
-            jax.ShapeDtypeStruct((parts, rows, slice_w), BF),
-            jax.ShapeDtypeStruct((parts, rows, slice_w), BF),
-            jax.ShapeDtypeStruct((rows, hidden), BF),
-            jax.ShapeDtypeStruct((rows, hidden), BF),
+            pltpu.VMEM((2 * n_tok, columns), BF),
+            pltpu.VMEM((n_tok, slice_w), BF),
+            pltpu.VMEM((width, hidden), BF),
+            pltpu.VMEM((hidden, width), BF),
         ),
         in_specs=[anywhere] * 5 + [vmem, smem, vmem],
-        out_specs=[vmem, vmem] + [anywhere] * 4,
+        out_specs=[vmem] * 4,
         scratch_shapes=[
             pltpu.VMEM((n_tok, slice_w), BF),
             pltpu.VMEM((n_tok, slice_w), BF),
@@ -710,12 +706,12 @@
             pltpu.VMEM((2, half, columns), BF),
             pltpu.VMEM((2, n_tok, columns), BF),
             pltpu.VMEM((2, n_tok, columns), BF),
-            pltpu.SemaphoreType.DMA((10,)),
+            pltpu.SemaphoreType.DMA((6,)),
             pltpu.SemaphoreType.DMA((sems,)),
             pltpu.SemaphoreType.DMA((sems,)),
         ],
         compiler_params=pltpu.CompilerParams(
-            collective_id=0, has_side_effects=True, vmem_limit_bytes=62 * 1024 * 1024
+            collective_id=0, has_side_effects=True, vmem_limit_bytes=50 * 1024 * 1024
         ),
         cost_estimate=pl.CostEstimate(
             flops=8 * 10**9, bytes_accessed=20 * 10**6, transcendentals=3 * 10**5
@@ -725,39 +721,24 @@
         tokens, upstream, w_in, w_out, flat,
         picked[:, 0, :], counts, combine[:, 0, :],
     )
-    products, grads, taken, row_grad, hid, preact_grad = out
-    whole = lambda shape: pl.BlockSpec(shape, lambda j: (0, 0))
-    slab = lambda *shape: pl.BlockSpec(shape, lambda j: (j, 0))
-    step, grad_step = 2 * n_tok // parts, n_tok // parts
-    grad_in, grad_out, projected, grad_tokens = pl.pallas_call(
-        weight_grad_kernel,
-        grid=(parts,),
+    products, grads, grad_in, grad_out = out
+    projected, grad_tokens, grad_in, grad_out = pl.pallas_call(
+        write_kernel,
         out_shape=(
+            jax.ShapeDtypeStruct((2 * n_tok * kinds * heads, lanes), BF),
+            jax.ShapeDtypeStruct((n_tok, slice_w), BF),
             jax.ShapeDtypeStruct(w_in.shape, BF),
             jax.ShapeDtypeStruct(w_out.shape, BF),
-            jax.ShapeDtypeStruct((2 * n_tok * kinds * heads, lanes), BF),
-            jax.ShapeDtypeStruct((n_tok, slice_w), BF),
         ),
-        in_specs=[
-            pl.BlockSpec((1, rows, slice_w), lambda j: (j, 0, 0)),
-            pl.BlockSpec((1, rows, slice_w), lambda j: (j, 0, 0)),
-            whole((rows, hidden)),
-            whole((rows, hidden)),
-            slab(step, columns),
-            slab(grad_step, slice_w),
-        ],
-        out_specs=(
-            pl.BlockSpec((1, slice_w, hidden), lambda j: (0, j, 0)),
-            pl.BlockSpec((1, hidden, slice_w), lambda j: (0, 0, j)),
-            slab(step * kinds * heads, lanes),
-            slab(grad_step, slice_w),
+        in_specs=[vmem] * 4,
+        out_specs=(vmem, anywhere, anywhere, anywhere),
+        scratch_shapes=[pltpu.SemaphoreType.DMA((3,))],
+        compiler_params=pltpu.CompilerParams(vmem_limit_bytes=16 * 1024 * 1024),
+        cost_estimate=pl.CostEstimate(
+            flops=2 * 10**8, bytes_accessed=18 * 10**6, transcendentals=0
         ),
-        compiler_params=pltpu.CompilerParams(vmem_limit_bytes=60 * 1024 * 1024),
-        cost_estimate=pl.CostEstimate(
-            flops=2 * 10**9, bytes_accessed=15 * 10**6, transcendentals=0
-        ),
-        name="weight_grads",
-    )(taken, row_grad, hid, preact_grad, products, grads)
+        name="write_out",
+    )(grad_in, grad_out, products, grads)
     projected = projected.reshape(2 * n_tok, kinds, heads, lanes).transpose(0, 2, 1, 3)
     return projected, grad_tokens, grad_in, grad_out
 

time: 124 us -> 119 us (0.960)
  Pallas kernels: 123 us -> 117 us
    pallas_call x2, Pallas kernels: 123 us -> 117 us  [the longest x1 113 us: on_device(): pl.pallas_call(layer_kernel, out_shape=(pltpu.VMEM((2 * n_tok, columns),...]
where the time goes in v3:
time: 119 us; the launch traced here: 118 us
  Pallas kernels  117 us (98%)
    pallas_call x1, Pallas kernels, on_device(): pl.pallas_call(layer_kernel, out_shape=(pltpu.VMEM((2 * n_tok, columns),...  113 us
    pallas_call x1, Pallas kernels, on_device(): pl.pallas_call(write_kernel, out_shape=(jax.ShapeDtypeStruct((2 * n_tok *...  4.36 us

profile of v3, /device:TPU:5, one launch (start us, length us, event | category | flops | bytes accessed | tf_op | source)
XLA Modules:
  0.0 118.3 jit_solution(13716750211426175835)
XLA Ops:
  0.6 113.1 %moe_layer.1 = (bf16[512,768]{1,0:T(8,128)(2,1)S(1)}, bf16[256,512]{1,0:T(8,128)(2,1)S(1)}, bf16[4096,512]{1,0:T(8,128)(2,1)S(1)}, bf16[512,4096]{1,0:T(8,128)(2,1)S(1)}) custom-call(bf16[256,4096]{1,0:T(8,128)(2,1)} %tokens.1, bf16[256,4096]{1,0:T(8,128)(2,1)} %upstream.1, bf16[1,4096,512]{2,1,0:T(8,128)(2,1)} %w_in.1, bf16[1,512,4096]{2,1,0:T(8,128)(2,1)} %w_out.1, ...), custom_call_target="tpu_custom_call" | custom-call | flops 8000000000 | bytes 20000000 | tf_op jit(solution)/shard_map/moe_layer/pallas_call | solution.py:662
  113.7 4.4 %write_out.1 = (bf16[3072,128]{1,0:T(8,128)(2,1)}, bf16[256,512]{1,0:T(8,128)(2,1)}, bf16[1,4096,512]{2,1,0:T(8,128)(2,1)}, bf16[1,512,4096]{2,1,0:T(8,128)(2,1)}) custom-call(bf16[4096,512]{1,0:T(8,128)(2,1)S(1)} %get-tuple-element.12.grad_in_v, bf16[512,4096]{1,0:T(8,128)(2,1)S(1)} %get-tuple-element.13.grad_out_v, ...), custom_call_target="tpu_custom_call" | custom-call | flops 200000000 | bytes 18000000 | tf_op jit(solution)/shard_map/write_out/pallas_call | solution.py:725

commit v4 on v3

--- a/solution.py
+++ b/solution.py
@@ -94,20 +94,21 @@
 def layer_kernel(
     tokens, upstream, w_in, w_out, w_qkv, picked, counts, combine,
     projected, grad_tokens, grad_in, grad_out,
-    tok, ups, ups_half, win, wout, wraw, wqkv, sel, comp, wcol,
+    tok, ups, ups_half, win, wout, wraw, wq, sel, comp, wcol,
     send_f, send_b, recv_f, recv_b, ag_f, ag_b,
     acc, slope, hid, pgr,
     pst, d2d, sbuf, half_l, half_r, full_l, full_r,
-    ret_s, ret_r, lay, stage, d2dp, hl, hr, fl, fr,
+    ret_s, ret_r, lay_s, lay, sum_p, sum_q, out_s,
     load_sems, send_sems, recv_sems,
 ):
     s, t = lax.axis_index("expert"), lax.axis_index("tensor")
     z, y = s // RING, s % RING
     x, c = t // 2, t % 2
-    shards, experts, cap = 16, counts.shape[0], combine.shape[1]
+    shards, parts = RING * RING, 2 * RING
+    experts, cap = counts.shape[0], combine.shape[1]
     n_tok, width = tok.shape
     half_rows = n_tok // 2
-    quarter = n_tok // 4
+    piece = n_tok // parts
 
     def wrap(v):
         return lax.rem(v + RING, RING)
@@ -146,10 +147,15 @@
         return carry
 
     lax.fori_loop(1, shards, greet, 0)
-    for device in (to_left, to_right, to_sib):
+
+    def greet_line(i, carry):
         pl.semaphore_signal(
-            barrier, inc=1, device_id=device, device_id_type=pl.DeviceIdType.MESH
+            barrier, inc=1, device_id=(s, lax.rem(t + i, parts)),
+            device_id_type=pl.DeviceIdType.MESH,
         )
+        return carry
+
+    lax.fori_loop(1, parts, greet_line, 0)
 
     slots = experts * cap
     lane = lax.broadcasted_iota(jnp.int32, (1, slots), 1)
@@ -174,7 +180,15 @@
     load_tok.wait()
     send_f[...] = dot(sel[...], tok[...], TN).astype(BF).reshape(send_f.shape)
 
-    pl.semaphore_wait(barrier, shards - 1 + 3)
+    load_qkv.wait()
+    blocks = wq.shape[2] // 128
+    turn = row_permutation(blocks, True)
+    for f in range(0, width, BAND):
+        moved = dot(turn, wraw[f * blocks:(f + BAND) * blocks, :]).astype(BF)
+        for k in range(blocks):
+            wq[t, f:f + BAND, k * 128:(k + 1) * 128] = moved[k * BAND:(k + 1) * BAND]
+
+    pl.semaphore_wait(barrier, shards - 1 + parts - 1)
 
     w = Wires(send_sems, recv_sems)
 
@@ -205,7 +219,56 @@
 
         lax.fori_loop(1, shards, body, 0)
 
+    class RowGather:
+        def __init__(self, buf, first, count):
+            self.buf = buf
+            self.whole = lambda block: buf.at[block, pl.ds(first, count), :]
+
+            def at(block, half):
+                return buf.at[block, pl.ds(first + half * count // 2, count // 2), :]
+
+            self.ring = RingGather(w, at, t, left, right, far, to_left, to_right)
+            self.base = w.take(7)
+            self.at = at
+
+        def give(self, k, ref):
+            w.send(self.base + k, ref, ref, to_sib)
+
+        def start(self):
+            self.ring.start()
+            self.give(0, self.whole(t))
+
+        def forward(self):
+            self.ring.forward()
+            self.give(1, self.at(left, 1))
+            self.give(2, self.at(right, 0))
+
+        def near(self):
+            self.ring.near()
+            self.give(3, self.at(left, 0))
+            self.give(4, self.at(right, 1))
+
+        def last(self):
+            self.ring.last()
+            self.give(5, self.at(far, 1))
+            self.give(6, self.at(far, 0))
+
+        def sib_own(self):
+            w.arrived(self.base, self.whole(sib), to_sib)
+
+        def sib_near(self):
+            other = 1 - 2 * c
+            for k, (block, half) in enumerate(((left, 1), (right, 0), (left, 0), (right, 1))):
+                w.arrived(self.base + 1 + k, self.at(block + other, half), to_sib)
+
+        def sib_last(self):
+            other = 1 - 2 * c
+            w.arrived(self.base + 5, self.at(far + other, 1), to_sib)
+            w.arrived(self.base + 6, self.at(far + other, 0), to_sib)
+
     ex_f = exchange(lambda to: send_f.at[to // 2], recv_f)
+    qkv_rows = [RowGather(wq, k * width // 2, width // 2) for k in range(2)]
+    qkv_rows[0].start()
 
     eye = (
         lax.broadcasted_iota(jnp.int32, (cap, cap), 0)
@@ -239,60 +302,6 @@
         part = slice(k * width, (k + 1) * width)
         taken = dot(sel[...], ups_half[:, part], TN) * wcol[...]
         send_b[:, :, part] = taken.astype(BF).reshape(experts, cap, width)
-
-    load_qkv.wait()
-    blocks = wqkv.shape[1] // 128
-    turn = row_permutation(blocks, True)
-    for f in range(0, width, BAND):
-        moved = dot(turn, wraw[f * blocks:(f + BAND) * blocks, :]).astype(BF)
-        for k in range(blocks):
-            wqkv[f:f + BAND, k * 128:(k + 1) * 128] = moved[k * BAND:(k + 1) * BAND]
-
-    class RowGather:
-        def __init__(self, buf):
-            self.buf = buf
-
-            def at(block, half):
-                return buf.at[block, pl.ds(half * half_rows, half_rows), :]
-
-            self.ring = RingGather(w, at, t, left, right, far, to_left, to_right)
-            self.base = w.take(7)
-            self.at = at
-
-        def give(self, k, ref):
-            w.send(self.base + k, ref, ref, to_sib)
-
-        def start(self):
-            self.ring.start()
-            self.give(0, self.buf.at[t])
-
-        def forward(self):
-            self.ring.forward()
-            self.give(1, self.at(left, 1))
-            self.give(2, self.at(right, 0))
-
-        def near(self):
-            self.ring.near()
-            self.give(3, self.at(left, 0))
-            self.give(4, self.at(right, 1))
-
-        def last(self):
-            self.ring.last()
-            self.give(5, self.at(far, 1))
-            self.give(6, self.at(far, 0))
-
-        def sib_own(self):
-            w.arrived(self.base, self.buf.at[sib], to_sib)
-
-        def sib_near(self):
-            other = 1 - 2 * c
-            for k, (block, half) in enumerate(((left, 1), (right, 0), (left, 0), (right, 1))):
-                w.arrived(self.base + 1 + k, self.at(block + other, half), to_sib)
-
-        def sib_last(self):
-            other = 1 - 2 * c
-            w.arrived(self.base + 5, self.at(far + other, 1), to_sib)
-            w.arrived(self.base + 6, self.at(far + other, 0), to_sib)
 
     other = 1 - 2 * c
 
@@ -385,12 +394,13 @@
         low = (values - high.astype(F32)).astype(BF)
         return dot(sel[...], high) + dot(sel[...], low)
 
-    gather_f = RowGather(ag_f)
+    gather_f = RowGather(ag_f, 0, n_tok)
     exchanged(ex_f, recv_f)
     ag_f[t] = dot(comp[...], recv_f[...].reshape(padded, width)).astype(BF)
     gather_f.start()
     ex_b = exchange(lambda to: send_b.at[to // 2], recv_b)
     gather_f.forward()
+    qkv_rows[0].forward()
     load_win.wait()
     gathered(gather_f, win_at, NN)
     pre = acc[...]
@@ -403,7 +413,10 @@
 
 
     reduce_f.forward()
+    qkv_rows[0].near()
+    qkv_rows[0].last()
     back_f = send_back(0, reduce_f.result())
+    qkv_rows[1].start()
 
     give_b = w.take(RING)
     exchanged(ex_b, recv_b)
@@ -424,23 +437,41 @@
     pgr[...] = (acc[...] * slope[...]).astype(BF)
     halves = returned(0, back_f)
     mixture = scatter(halves * wcol[...])
-    lay[s] = (tok[...].astype(F32) + mixture).astype(BF)
-
-    def lay_at(part, along_z, fixed):
+    layer = (tok[...].astype(F32) + mixture).astype(BF)
+    lay_s[...] = layer.reshape(lay_s.shape)
+    line_base = w.take(parts)
+
+    def to_line(i, carry):
+        to = lax.rem(t + i, parts)
+        w.send(line_base + i, lay_s.at[to], lay.at[z, y, t], (s, to), keep=False)
+        return carry
+
+    def from_line(i, carry):
+        source = lax.rem(t - i + parts, parts)
+        w.arrived(line_base + i, lay.at[z, y, source], (s, source))
+        return carry
+
+    def line_end(i, carry):
+        w.copy(line_base + i, lay_s.at[0], lay_s.at[0], to_sib).wait_send()
+        return carry
+
+    lax.fori_loop(1, parts, to_line, 0)
+    lay[z, y, t] = lay_s[t]
+    qkv_rows[1].forward()
+
+    reduce_b = RowReduce(1)
+    reduce_b.partials(pgr, win_at, NT)
+    lax.fori_loop(1, parts, from_line, 0)
+
+    def along_y(part, zz):
         def at(pos, half):
-            index = pos * RING + fixed if along_z else fixed + pos
-            return lay.at[index, pl.ds(part * half_rows + half * quarter, quarter), :]
-        return at
-
-    def along_y(part, zz):
-        return RingGather(
-            w, lay_at(part, False, zz * RING), y, y_minus, y_plus, y_far, to_ym, to_yp
-        )
+            return lay.at[zz, pos, pl.ds(part * RING + half * 2, 2)]
+        return RingGather(w, at, y, y_minus, y_plus, y_far, to_ym, to_yp)
 
     def along_z(part, yy):
-        return RingGather(
-            w, lay_at(part, True, yy), z, z_minus, z_plus, z_far, to_zm, to_zp
-        )
+        def at(pos, half):
+            return lay.at[pos, yy, pl.ds(part * RING + half * 2, 2)]
+        return RingGather(w, at, z, z_minus, z_plus, z_far, to_zm, to_zp)
 
     first_p, first_q = along_y(0, z), along_z(1, y)
     second_p = [along_z(0, yy) for yy in (y, y_minus, y_plus, y_far)]
@@ -450,78 +481,45 @@
     second_p[0].start()
     second_q[0].start()
 
-    reduce_b = RowReduce(1)
-    reduce_b.partials(pgr, win_at, NT)
-
-    unit_base = w.take(8)
-    x_base = w.take(12)
-
-    def unit(q, zp, cp):
-        for i in range(2):
-            block = lay[zp * RING + cp * 2 + i, q * half_rows:(q + 1) * half_rows, :]
-            stage[q, cp, zp, i * half_rows:(i + 1) * half_rows, :] = dot(
-                block, wqkv[...]
-            ).astype(BF)
-
-        @pl.when(cp != c)
+    rows_of_four = RING * piece
+
+    def products(blocks_at, first):
+        total = None
+        for k in range(first, first + RING):
+            term = dot(blocks_at(k).reshape(rows_of_four, width), wq[k])
+            total = term if total is None else total + term
+        return total.reshape(RING, piece, -1)
+
+    def group_p(zz):
+        sum_p[zz] = products(lambda k: lay[zz, :, k], 0)
+
+    def group_q(yy):
+        sum_q[:, yy] = products(lambda k: lay[:, yy, k], RING)
+
+    out_base = w.take(2 * parts)
+
+    def out_copy(zz, yy):
+        to = zz * 2 + yy // 2
+        return to, pltpu.make_async_remote_copy(
+            src_ref=out_s.at[zz, yy],
+            dst_ref=projected.at[lax.rem(yy, 2), t],
+            send_sem=send_sems.at[out_base + zz * RING + yy],
+            recv_sem=recv_sems.at[out_base + lax.rem(yy, 2) * parts + t],
+            device_id=(s, to),
+            device_id_type=pl.DeviceIdType.MESH,
+        )
+
+    def deliver(zz, yy):
+        out_s[zz, yy] = (sum_p[zz, yy] + sum_q[zz, yy]).astype(BF)
+        to, copy = out_copy(zz, yy)
+
+        @pl.when(to != t)
         def _():
-            w.send(
-                unit_base + q * RING + zp, stage.at[q, cp, zp], d2dp.at[q, zp], to_sib,
-                keep=False,
-            )
-
-    lo, hi = pl.ds(0, half_rows), pl.ds(half_rows, half_rows)
-
-    def settle(q, zp):
-        b = x_base + q * 6
-        w.arrived(unit_base + q * RING + zp, d2dp.at[q, zp], to_sib)
-        stage[q, c, zp] = (
-            stage[q, c, zp].astype(F32) + d2dp[q, zp].astype(F32)
-        ).astype(BF)
-        d = wrap(zp - x)
-
-        @pl.when(d == 2)
+            copy.start()
+
+        @pl.when(to == t)
         def _():
-            w.send(b, stage.at[q, c, zp, hi], hl.at[q], to_right, keep=False)
-            w.send(b + 1, stage.at[q, c, zp, lo], hr.at[q], to_left, keep=False)
-
-        @pl.when(d == 1)
-        def _():
-            w.send(b + 2, stage.at[q, c, zp, lo], fl.at[q, lo], to_right, keep=False)
-
-        @pl.when(d == 3)
-        def _():
-            w.send(b + 3, stage.at[q, c, zp, hi], fr.at[q, hi], to_left, keep=False)
-
-    def pass_on(q):
-        b = x_base + q * 6
-        zr, zl = wrap(x + 1), wrap(x - 1)
-        w.arrived(b, hl.at[q], to_right)
-        stage[q, c, zr, hi] = (
-            stage[q, c, zr, hi].astype(F32) + hl[q].astype(F32)
-        ).astype(BF)
-        w.send(b + 4, stage.at[q, c, zr, hi], fl.at[q, hi], to_right, keep=False)
-        w.arrived(b + 1, hr.at[q], to_left)
-        stage[q, c, zl, lo] = (
-            stage[q, c, zl, lo].astype(F32) + hr[q].astype(F32)
-        ).astype(BF)
-        w.send(b + 5, stage.at[q, c, zl, lo], fr.at[q, lo], to_left, keep=False)
-
-    def finish(q):
-        b = x_base + q * 6
-        w.arrived(b + 2, fl.at[q, lo], to_right)
-        w.arrived(b + 3, fr.at[q, hi], to_left)
-        w.arrived(b + 4, fl.at[q, hi], to_right)
-        w.arrived(b + 5, fr.at[q, lo], to_left)
-        total = (
-            stage[q, c, x].astype(F32) + fl[q].astype(F32) + fr[q].astype(F32)
-        ).astype(BF)
-        for i in range(2):
-            first = i * n_tok + q * half_rows
-            projected[first:first + half_rows, :] = total[i * half_rows:(i + 1) * half_rows]
-
-    z_order = (z, z_plus, z_minus, z_far)
-    pair = y // 2
+            projected[lax.rem(yy, 2), t] = out_s[zz, yy]
 
     first_p.forward()
     first_q.forward()
@@ -532,84 +530,75 @@
     for k in (1, 2):
         second_p[k].start()
         second_q[k].start()
-    second_q[0].near()
-    unit(0, z, pair)
-    unit(1, z, pair)
+    reduce_b.forward()
+    qkv_rows[1].near()
+    qkv_rows[1].last()
     first_p.last()
     first_q.last()
     second_p[3].start()
     second_q[3].start()
-    unit(0, z, 1 - pair)
     for k in (1, 2):
         second_p[k].forward()
         second_q[k].forward()
-    reduce_b.forward()
-    settle(0, z)
-
-    @pl.when(pair == c)
-    def _():
-        settle(1, z)
-
-    for j in range(2 * RING):
-        part = slice(j * width, (j + 1) * width)
-        grad_in[part, :] = dot(ag_f[j], pgr[...], TN).astype(BF)
-    for k in (1, 2):
-        second_q[k].near()
-    unit(1, z_plus, pair)
-    unit(1, z_minus, pair)
+    for gather in qkv_rows:
+        gather.sib_own()
+        gather.sib_near()
+        gather.sib_last()
+    group_p(z)
+    group_q(y)
     second_p[3].forward()
     second_q[3].forward()
     back_b = send_back(1, reduce_b.result())
-    second_q[3].near()
-    unit(1, z_far, pair)
+    for j in range(parts):
+        part = slice(j * width, (j + 1) * width)
+        grad_in[part, :] = dot(ag_f[j], pgr[...], TN).astype(BF)
+    for k in range(RING):
+        second_p[k].near()
+        second_q[k].near()
+    group_p(z_plus)
+    group_q(y_plus)
+    group_p(z_minus)
+    group_q(y_minus)
+    for zz in (z_plus, z_minus, z):
+        for yy in (y_plus, y_minus, y):
+            deliver(zz, yy)
     hid_turned = hid[...].T
-    for j in range(2 * RING):
+    for j in range(parts):
         part = slice(j * width, (j + 1) * width)
         grad_out[:, part] = dot(hid_turned, ag_b[j]).astype(BF)
-    for k in range(4):
-        second_p[k].near()
-    for zp in (z_plus, z_minus):
-        unit(0, zp, 0)
-        unit(0, zp, 1)
-
-    @pl.when(pair == c)
-    def _():
-        for zp in (z_plus, z_minus, z_far):
-            settle(1, zp)
-
-    for zp in (z_plus, z_minus):
-        settle(0, zp)
-    for k in range(4):
-        second_p[k].last()
-    unit(0, z_far, 0)
-    unit(0, z_far, 1)
-    for k in range(4):
-        second_q[k].last()
-    for zp in z_order:
-        unit(1, zp, 1 - pair)
-    settle(0, z_far)
-
-    @pl.when(pair == c)
-    def _():
-        pass_on(1)
-
-    pass_on(0)
-
-    @pl.when(pair != c)
-    def _():
-        for zp in z_order:
-            settle(1, zp)
-
     load_ups.wait()
     back_rows = scatter(returned(1, back_b))
     grad_tokens[...] = (ups[...].astype(F32) + back_rows).astype(BF)
-
-    @pl.when(pair != c)
-    def _():
-        pass_on(1)
-
-    finish(0)
-    finish(1)
+    for k in range(RING):
+        second_p[k].last()
+    group_p(z_far)
+    for yy in (y_plus, y_minus, y):
+        deliver(z_far, yy)
+    for k in range(RING):
+        second_q[k].last()
+    group_q(y_far)
+    for zz in (z_far, z_plus, z_minus, z):
+        deliver(zz, y_far)
+
+    def out_end(i, carry):
+        to, copy = out_copy(i // RING, lax.rem(i, RING))
+
+        @pl.when(to != t)
+        def _():
+            copy.wait_send()
+
+        return carry
+
+    def out_arrived(i, carry):
+        source = lax.rem(t - i + parts, parts)
+        for shard in range(2):
+            slot = out_base + shard * parts + source
+            w.arrived(slot, projected.at[shard, source], (s, source))
+        return carry
+
+    lax.fori_loop(1, parts, out_arrived, 0)
+    lax.fori_loop(0, shards, out_end, 0)
+    lax.fori_loop(1, parts, line_end, 0)
 
     for copy in w.sent:
         copy.wait_send()
@@ -617,12 +606,6 @@
     exchange_end(ex_b, recv_b)
     exchange_end(back_f, ret_r.at[0])
     exchange_end(back_b, ret_r.at[1])
-
-    for q in range(2):
-        for k in range(RING):
-            w.copy(unit_base + q * RING + k, d2dp.at[q, k], d2dp.at[q, k], to_sib).wait_send()
-        for k in range(6):
-            w.copy(x_base + q * 6 + k, hl.at[q], hl.at[q], to_left).wait_send()
 
 
 def write_kernel(
@@ -654,7 +637,6 @@
     heads, kinds, lanes = w_qkv.shape[1:]
     columns = heads * kinds * lanes
     flat = w_qkv.transpose(0, 2, 1, 3).reshape(slice_w * kinds * heads, lanes)
-    half = n_tok // 2
     anywhere = pl.BlockSpec(memory_space=pl.ANY)
     vmem = pl.BlockSpec(memory_space=pltpu.VMEM)
     smem = pl.BlockSpec(memory_space=pltpu.SMEM)
@@ -662,7 +644,7 @@
     out = pl.pallas_call(
         layer_kernel,
         out_shape=(
-            pltpu.VMEM((2 * n_tok, columns), BF),
+            pltpu.VMEM((2, parts, n_tok // parts, columns), BF),
             pltpu.VMEM((n_tok, slice_w), BF),
             pltpu.VMEM((width, hidden), BF),
             pltpu.VMEM((hidden, width), BF),
@@ -676,7 +658,7 @@
             pltpu.VMEM((width, hidden), BF),
             pltpu.VMEM((hidden, width), BF),
             pltpu.VMEM(flat.shape, BF),
-            pltpu.VMEM((slice_w, columns), BF),
+            pltpu.VMEM((parts, slice_w, columns), BF),
             pltpu.VMEM((n_tok, rows), BF),
             pltpu.VMEM((rows, shards * cap), BF),
             pltpu.VMEM((rows, 1), F32),
@@ -699,13 +681,11 @@
             pltpu.VMEM((2, rows, slice_w), BF),
             pltpu.VMEM((2, shards, cap, slice_w), BF),
             pltpu.VMEM((2, shards, cap, slice_w), BF),
-            pltpu.VMEM((shards, n_tok, slice_w), BF),
-            pltpu.VMEM((2, 2, RING, n_tok, columns), BF),
-            pltpu.VMEM((2, RING, n_tok, columns), BF),
-            pltpu.VMEM((2, half, columns), BF),
-            pltpu.VMEM((2, half, columns), BF),
-            pltpu.VMEM((2, n_tok, columns), BF),
-            pltpu.VMEM((2, n_tok, columns), BF),
+            pltpu.VMEM((parts, n_tok // parts, slice_w), BF),
+            pltpu.VMEM((RING, RING, parts, n_tok // parts, slice_w), BF),
+            pltpu.VMEM((RING, RING, n_tok // parts, columns), F32),
+            pltpu.VMEM((RING, RING, n_tok // parts, columns), F32),
+            pltpu.VMEM((RING, RING, n_tok // parts, columns), BF),
             pltpu.SemaphoreType.DMA((6,)),
             pltpu.SemaphoreType.DMA((sems,)),
             pltpu.SemaphoreType.DMA((sems,)),
@@ -738,7 +718,7 @@
             flops=2 * 10**8, bytes_accessed=18 * 10**6, transcendentals=0
         ),
         name="write_out",
-    )(grad_in, grad_out, products, grads)
+    )(grad_in, grad_out, products.reshape(2 * n_tok, columns), grads)
     projected = projected.reshape(2 * n_tok, kinds, heads, lanes).transpose(0, 2, 1, 3)
     return projected, grad_tokens, grad_in, grad_out
 

time: 119 us -> 112 us (0.941)
  Pallas kernels: 117 us -> 111 us
    pallas_call x1, Pallas kernels: 113 us -> 107 us  [on_device(): pl.pallas_call(layer_kernel, out_shape=(pltpu.VMEM((2, parts, n_tok // pa...]
where the time goes in v4:
time: 112 us
  Pallas kernels  111 us (99%)
    pallas_call x1, Pallas kernels, on_device(): pl.pallas_call(layer_kernel, out_shape=(pltpu.VMEM((2, parts, n_tok // pa...  107 us
    pallas_call x1, Pallas kernels, on_device(): pl.pallas_call(write_kernel, out_shape=(jax.ShapeDtypeStruct((2 * n_tok *...  4.36 us

profile of v4, /device:TPU:5, one launch (start us, length us, event | category | flops | bytes accessed | tf_op | source)
XLA Modules:
  0.0 111.8 jit_solution(9667917598719538926)
XLA Ops:
  0.6 106.6 %moe_layer.1 = (bf16[2,8,32,768]{3,2,1,0:T(8,128)(2,1)S(1)}, bf16[256,512]{1,0:T(8,128)(2,1)S(1)}, bf16[4096,512]{1,0:T(8,128)(2,1)S(1)}, bf16[512,4096]{1,0:T(8,128)(2,1)S(1)}) custom-call(bf16[256,4096]{1,0:T(8,128)(2,1)} %tokens.1, bf16[256,4096]{1,0:T(8,128)(2,1)} %upstream.1, bf16[1,4096,512]{2,1,0:T(8,128)(2,1)} %w_in.1, bf16[1,512,4096]{2,1,0:T(8,128)(2,1)} %w_out.1, ...), custom_call_target="tpu_custom_call" | custom-call | flops 8000000000 | bytes 20000000 | tf_op jit(solution)/shard_map/moe_layer/pallas_call | solution.py:644
  107.3 4.4 %write_out.1 = (bf16[3072,128]{1,0:T(8,128)(2,1)}, bf16[256,512]{1,0:T(8,128)(2,1)}, bf16[1,4096,512]{2,1,0:T(8,128)(2,1)}, bf16[1,512,4096]{2,1,0:T(8,128)(2,1)}) custom-call(bf16[4096,512]{1,0:T(8,128)(2,1)S(1)} %get-tuple-element.12.grad_in_v, bf16[512,4096]{1,0:T(8,128)(2,1)S(1)} %get-tuple-element.13.grad_out_v, bf16[512,768]{1,0:T(8,128)(2,1)S(1)} %bitcast.9, ...), custom_call_target="tpu_custom_call" | custom-call | flops 200000000 | bytes 18000000 | tf_op jit(solution)/shard_map/write_out/pallas_call | solution.py:705

commit v5 on v4

--- a/solution.py
+++ b/solution.py
@@ -12,6 +12,10 @@
 TN = (((0,), (0,)), ((), ()))
 RING = 4
 BAND = 32
+OFFSETS = sorted(
+    ((dz, dy) for dz in range(RING) for dy in range(RING) if dz or dy),
+    key=lambda step: -sum(min(d, RING - d) for d in step),
+)
 
 
 def dot(a, b, dims=NN):
@@ -65,30 +69,33 @@
         self.to_minus, self.to_plus = to_minus, to_plus
         self.base = wires.take(6)
 
-    def start(self):
+    def start(self, half):
+        ref, b = self.at(self.me, half), self.base
+        self.w.send(b + 1 - half, ref, ref, self.to_plus)
+        self.w.send(b + 3 + half, ref, ref, self.to_minus)
+
+    def forward(self, half):
         b = self.base
-        for i, half in enumerate((1, 0)):
-            ref = self.at(self.me, half)
-            self.w.send(b + i, ref, ref, self.to_plus)
-            ref = self.at(self.me, 1 - half)
-            self.w.send(b + 3 + i, ref, ref, self.to_minus)
-
-    def forward(self):
-        b = self.base
-        ref = self.at(self.minus, 1)
-        self.w.arrived(b, ref, self.to_plus)
-        self.w.send(b + 2, ref, ref, self.to_plus)
-        ref = self.at(self.plus, 0)
-        self.w.arrived(b + 3, ref, self.to_minus)
-        self.w.send(b + 5, ref, ref, self.to_minus)
-
-    def near(self):
-        self.w.arrived(self.base + 1, self.at(self.minus, 0), self.to_plus)
-        self.w.arrived(self.base + 4, self.at(self.plus, 1), self.to_minus)
-
-    def last(self):
-        self.w.arrived(self.base + 2, self.at(self.far, 1), self.to_plus)
-        self.w.arrived(self.base + 5, self.at(self.far, 0), self.to_minus)
+        if half:
+            ref = self.at(self.minus, 1)
+            self.w.arrived(b, ref, self.to_plus)
+            self.w.send(b + 2, ref, ref, self.to_plus)
+        else:
+            ref = self.at(self.plus, 0)
+            self.w.arrived(b + 3, ref, self.to_minus)
+            self.w.send(b + 5, ref, ref, self.to_minus)
+
+    def near(self, half):
+        if half:
+            self.w.arrived(self.base + 4, self.at(self.plus, 1), self.to_minus)
+        else:
+            self.w.arrived(self.base + 1, self.at(self.minus, 0), self.to_plus)
+
+    def last(self, half):
+        if half:
+            self.w.arrived(self.base + 2, self.at(self.far, 1), self.to_plus)
+        else:
+            self.w.arrived(self.base + 5, self.at(self.far, 0), self.to_minus)
 
 
 def layer_kernel(
@@ -131,12 +138,6 @@
     load_half = pltpu.make_async_copy(upstream.at[:, wide_cols], ups_half, load_sems.at[4])
     load_qkv = pltpu.make_async_copy(w_qkv, wraw, load_sems.at[5])
     load_tok.start()
-    load_half.start()
-    load_win.start()
-    load_wout.start()
-    load_qkv.start()
-    load_ups.start()
-
     barrier = pltpu.get_barrier_semaphore()
 
     def greet(i, carry):
@@ -156,6 +157,12 @@
         return carry
 
     lax.fori_loop(1, parts, greet_line, 0)
+
+    load_half.start()
+    load_win.start()
+    load_wout.start()
+    load_qkv.start()
+    load_ups.start()
 
     slots = experts * cap
     lane = lax.broadcasted_iota(jnp.int32, (1, slots), 1)
@@ -180,6 +187,85 @@
     load_tok.wait()
     send_f[...] = dot(sel[...], tok[...], TN).astype(BF).reshape(send_f.shape)
 
+    pl.semaphore_wait(barrier, shards - 1 + parts - 1)
+
+    w = Wires(send_sems, recv_sems)
+
+    def exchange(src_at, recv):
+        base = w.take(shards)
+
+        for dz, dy in OFFSETS:
+            to = wrap(z + dz) * RING + wrap(y + dy)
+            w.send(base + dz * RING + dy, src_at(to), recv.at[s], (to, t), keep=False)
+        recv[s] = src_at(s)[...]
+        return base
+
+    def exchanged(base, recv):
+        for dz, dy in OFFSETS:
+            source = wrap(z - dz) * RING + wrap(y - dy)
+            w.arrived(base + dz * RING + dy, recv.at[source], (source, t))
+
+    def exchange_end(base, recv):
+        def body(i, carry):
+            w.copy(base + i, recv.at[0], recv.at[0], to_sib).wait_send()
+            return carry
+
+        lax.fori_loop(1, shards, body, 0)
+
+    class RowGather:
+        def __init__(self, buf, first, count):
+            self.buf = buf
+            self.whole = lambda block: buf.at[block, pl.ds(first, count), :]
+
+            def at(block, half):
+                return buf.at[block, pl.ds(first + half * count // 2, count // 2), :]
+
+            self.ring = RingGather(w, at, t, left, right, far, to_left, to_right)
+            self.base = w.take(7)
+            self.at = at
+
+        def give(self, k, ref):
+            w.send(self.base + k, ref, ref, to_sib)
+
+        def start(self):
+            self.ring.start(1)
+            self.ring.start(0)
+            self.give(0, self.whole(t))
+
+        def forward(self):
+            self.ring.forward(1)
+            self.ring.forward(0)
+            self.give(1, self.at(left, 1))
+            self.give(2, self.at(right, 0))
+
+        def near(self):
+            self.ring.near(0)
+            self.ring.near(1)
+            self.give(3, self.at(left, 0))
+            self.give(4, self.at(right, 1))
+
+        def last(self):
+            self.ring.last(1)
+            self.ring.last(0)
+            self.give(5, self.at(far, 1))
+            self.give(6, self.at(far, 0))
+
+        def sib_own(self):
+            w.arrived(self.base, self.whole(sib), to_sib)
+
+        def sib_near(self):
+            other = 1 - 2 * c
+            for k, (block, half) in enumerate(((left, 1), (right, 0), (left, 0), (right, 1))):
+                w.arrived(self.base + 1 + k, self.at(block + other, half), to_sib)
+
+        def sib_last(self):
+            other = 1 - 2 * c
+            w.arrived(self.base + 5, self.at(far + other, 1), to_sib)
+            w.arrived(self.base + 6, self.at(far + other, 0), to_sib)
+
+    ex_f = exchange(lambda to: send_f.at[to // 2], recv_f)
+    part_rows = (5 * width // 16, 6 * width // 16, 5 * width // 16)
+    qkv_rows = [RowGather(wq, sum(part_rows[:k]), n) for k, n in enumerate(part_rows)]
     load_qkv.wait()
     blocks = wq.shape[2] // 128
     turn = row_permutation(blocks, True)
@@ -188,86 +274,6 @@
         for k in range(blocks):
             wq[t, f:f + BAND, k * 128:(k + 1) * 128] = moved[k * BAND:(k + 1) * BAND]
 
-    pl.semaphore_wait(barrier, shards - 1 + parts - 1)
-
-    w = Wires(send_sems, recv_sems)
-
-    def exchange(src_at, recv):
-        base = w.take(shards)
-
-        def body(i, carry):
-            to = lax.rem(s + i, shards)
-            w.send(base + i, src_at(to), recv.at[s], (to, t), keep=False)
-            return carry
-
-        lax.fori_loop(1, shards, body, 0)
-        recv[s] = src_at(s)[...]
-        return base
-
-    def exchanged(base, recv):
-        def body(i, carry):
-            source = lax.rem(s - i + shards, shards)
-            w.arrived(base + i, recv.at[source], (source, t))
-            return carry
-
-        lax.fori_loop(1, shards, body, 0)
-
-    def exchange_end(base, recv):
-        def body(i, carry):
-            w.copy(base + i, recv.at[0], recv.at[0], to_sib).wait_send()
-            return carry
-
-        lax.fori_loop(1, shards, body, 0)
-
-    class RowGather:
-        def __init__(self, buf, first, count):
-            self.buf = buf
-            self.whole = lambda block: buf.at[block, pl.ds(first, count), :]
-
-            def at(block, half):
-                return buf.at[block, pl.ds(first + half * count // 2, count // 2), :]
-
-            self.ring = RingGather(w, at, t, left, right, far, to_left, to_right)
-            self.base = w.take(7)
-            self.at = at
-
-        def give(self, k, ref):
-            w.send(self.base + k, ref, ref, to_sib)
-
-        def start(self):
-            self.ring.start()
-            self.give(0, self.whole(t))
-
-        def forward(self):
-            self.ring.forward()
-            self.give(1, self.at(left, 1))
-            self.give(2, self.at(right, 0))
-
-        def near(self):
-            self.ring.near()
-            self.give(3, self.at(left, 0))
-            self.give(4, self.at(right, 1))
-
-        def last(self):
-            self.ring.last()
-            self.give(5, self.at(far, 1))
-            self.give(6, self.at(far, 0))
-
-        def sib_own(self):
-            w.arrived(self.base, self.whole(sib), to_sib)
-
-        def sib_near(self):
-            other = 1 - 2 * c
-            for k, (block, half) in enumerate(((left, 1), (right, 0), (left, 0), (right, 1))):
-                w.arrived(self.base + 1 + k, self.at(block + other, half), to_sib)
-
-        def sib_last(self):
-            other = 1 - 2 * c
-            w.arrived(self.base + 5, self.at(far + other, 1), to_sib)
-            w.arrived(self.base + 6, self.at(far + other, 0), to_sib)
-
-    ex_f = exchange(lambda to: send_f.at[to // 2], recv_f)
-    qkv_rows = [RowGather(wq, k * width // 2, width // 2) for k in range(2)]
     qkv_rows[0].start()
 
     eye = (
@@ -446,55 +452,64 @@
         w.send(line_base + i, lay_s.at[to], lay.at[z, y, t], (s, to), keep=False)
         return carry
 
-    def from_line(i, carry):
-        source = lax.rem(t - i + parts, parts)
-        w.arrived(line_base + i, lay.at[z, y, source], (s, source))
-        return carry
-
     def line_end(i, carry):
         w.copy(line_base + i, lay_s.at[0], lay_s.at[0], to_sib).wait_send()
         return carry
 
     lax.fori_loop(1, parts, to_line, 0)
     lay[z, y, t] = lay_s[t]
-    qkv_rows[1].forward()
-
-    reduce_b = RowReduce(1)
-    reduce_b.partials(pgr, win_at, NT)
-    lax.fori_loop(1, parts, from_line, 0)
+
+    def from_chip(chip):
+        for core in range(2):
+            source = chip * 2 + core
+            w.arrived(
+                line_base + lax.rem(t - source + parts, parts), lay.at[z, y, source], (s, source)
+            )
+
+    chips = ((x, wrap(x + 2)), (wrap(x + 1), wrap(x - 1)))
 
     def along_y(part, zz):
         def at(pos, half):
-            return lay.at[zz, pos, pl.ds(part * RING + half * 2, 2)]
+            return lay.at[zz, pos, pl.ds(chips[part][half] * 2, 2)]
         return RingGather(w, at, y, y_minus, y_plus, y_far, to_ym, to_yp)
 
     def along_z(part, yy):
         def at(pos, half):
-            return lay.at[pos, yy, pl.ds(part * RING + half * 2, 2)]
+            return lay.at[pos, yy, pl.ds(chips[part][half] * 2, 2)]
         return RingGather(w, at, z, z_minus, z_plus, z_far, to_zm, to_zp)
 
     first_p, first_q = along_y(0, z), along_z(1, y)
     second_p = [along_z(0, yy) for yy in (y, y_minus, y_plus, y_far)]
     second_q = [along_y(1, zz) for zz in (z, z_minus, z_plus, z_far)]
-    first_p.start()
-    first_q.start()
-    second_p[0].start()
-    second_q[0].start()
+    w.arrived(line_base + lax.rem(t - sib + parts, parts), lay.at[z, y, sib], to_sib)
+    first_p.start(0)
+    second_p[0].start(0)
+    reduce_b = RowReduce(1)
+    reduce_b.partials(pgr, win_at, NT)
+    for half in (0, 1):
+        from_chip(chips[1][half])
+        first_q.start(half)
+        second_q[0].start(half)
+    from_chip(chips[0][1])
+    first_p.start(1)
+    second_p[0].start(1)
 
     rows_of_four = RING * piece
 
-    def products(blocks_at, first):
+    def products(blocks_at, part):
         total = None
-        for k in range(first, first + RING):
-            term = dot(blocks_at(k).reshape(rows_of_four, width), wq[k])
-            total = term if total is None else total + term
+        for half in range(2):
+            for core in range(2):
+                k = chips[part][half] * 2 + core
+                term = dot(blocks_at(k).reshape(rows_of_four, width), wq[k])
+                total = term if total is None else total + term
         return total.reshape(RING, piece, -1)
 
     def group_p(zz):
         sum_p[zz] = products(lambda k: lay[zz, :, k], 0)
 
     def group_q(yy):
-        sum_q[:, yy] = products(lambda k: lay[:, yy, k], RING)
+        sum_q[:, yy] = products(lambda k: lay[:, yy, k], 1)
 
     out_base = w.take(2 * parts)
 
@@ -521,64 +536,89 @@
         def _():
             projected[lax.rem(yy, 2), t] = out_s[zz, yy]
 
-    first_p.forward()
-    first_q.forward()
-    second_p[0].forward()
-    second_q[0].forward()
-    first_p.near()
-    first_q.near()
+    first_p.forward(0)
+    second_p[0].forward(0)
+    first_p.near(0)
     for k in (1, 2):
-        second_p[k].start()
-        second_q[k].start()
+        second_p[k].start(0)
+    qkv_rows[1].forward()
+    qkv_rows[2].start()
+    for half in (0, 1):
+        first_q.forward(half)
+        second_q[0].forward(half)
+    for half in (0, 1):
+        first_q.near(half)
+        for k in (1, 2):
+            second_q[k].start(half)
+    first_p.forward(1)
+    second_p[0].forward(1)
+    first_p.near(1)
+    first_p.last(0)
+    for k in (1, 2):
+        second_p[k].start(1)
+    second_p[3].start(0)
+    for k in (1, 2):
+        second_p[k].forward(0)
+    for half in (0, 1):
+        first_q.last(half)
+        second_q[3].start(half)
+    first_p.last(1)
+    second_p[3].start(1)
     reduce_b.forward()
-    qkv_rows[1].near()
-    qkv_rows[1].last()
-    first_p.last()
-    first_q.last()
-    second_p[3].start()
-    second_q[3].start()
     for k in (1, 2):
-        second_p[k].forward()
-        second_q[k].forward()
+        for half in (0, 1):
+            second_q[k].forward(half)
+        second_p[k].forward(1)
+    qkv_rows[2].forward()
+    second_p[3].forward(0)
+    for half in (0, 1):
+        second_q[3].forward(half)
+    second_p[3].forward(1)
+    for gather in qkv_rows[1:]:
+        gather.near()
+        gather.last()
+    back_b = send_back(1, reduce_b.result())
     for gather in qkv_rows:
         gather.sib_own()
         gather.sib_near()
         gather.sib_last()
     group_p(z)
     group_q(y)
-    second_p[3].forward()
-    second_q[3].forward()
-    back_b = send_back(1, reduce_b.result())
+    deliver(z, y)
+    for k in range(RING):
+        for half in (0, 1):
+            second_p[k].near(half)
+            second_q[k].near(half)
+    group_p(z_plus)
+    group_p(z_minus)
+    deliver(z_plus, y)
+    deliver(z_minus, y)
+    group_q(y_plus)
+    group_q(y_minus)
+    for zz in (z_plus, z_minus, z):
+        for yy in (y_plus, y_minus):
+            deliver(zz, yy)
+    for k in range(RING):
+        second_p[k].last(0)
+        second_p[k].last(1)
+    group_p(z_far)
+    for yy in (y_plus, y_minus, y):
+        deliver(z_far, yy)
+    for k in range(RING):
+        second_q[k].last(0)
+        second_q[k].last(1)
+    group_q(y_far)
+    for zz in (z_far, z_plus, z_minus, z):
+        deliver(zz, y_far)
+
+    hid_turned = hid[...].T
     for j in range(parts):
         part = slice(j * width, (j + 1) * width)
         grad_in[part, :] = dot(ag_f[j], pgr[...], TN).astype(BF)
-    for k in range(RING):
-        second_p[k].near()
-        second_q[k].near()
-    group_p(z_plus)
-    group_q(y_plus)
-    group_p(z_minus)
-    group_q(y_minus)
-    for zz in (z_plus, z_minus, z):
-        for yy in (y_plus, y_minus, y):
-            deliver(zz, yy)
-    hid_turned = hid[...].T
-    for j in range(parts):
-        part = slice(j * width, (j + 1) * width)
         grad_out[:, part] = dot(hid_turned, ag_b[j]).astype(BF)
     load_ups.wait()
     back_rows = scatter(returned(1, back_b))
     grad_tokens[...] = (ups[...].astype(F32) + back_rows).astype(BF)
-    for k in range(RING):
-        second_p[k].last()
-    group_p(z_far)
-    for yy in (y_plus, y_minus, y):
-        deliver(z_far, yy)
-    for k in range(RING):
-        second_q[k].last()
-    group_q(y_far)
-    for zz in (z_far, z_plus, z_minus, z):
-        deliver(zz, y_far)
 
     def out_end(i, carry):
         to, copy = out_copy(i // RING, lax.rem(i, RING))

time: 112 us -> 106 us (0.946)
  Pallas kernels: 111 us -> 105 us
    pallas_call x1, Pallas kernels: 107 us -> 100 us  [on_device(): pl.pallas_call(layer_kernel, out_shape=(pltpu.VMEM((2, parts, n_tok // pa...]
where the time goes in v5:
time: 106 us
  Pallas kernels  105 us (99%)
    pallas_call x1, Pallas kernels, on_device(): pl.pallas_call(layer_kernel, out_shape=(pltpu.VMEM((2, parts, n_tok // pa...  100 us
    pallas_call x1, Pallas kernels, on_device(): pl.pallas_call(write_kernel, out_shape=(jax.ShapeDtypeStruct((2 * n_tok *...  4.36 us

profile of v5, /device:TPU:5, one launch (start us, length us, event | category | flops | bytes accessed | tf_op | source)
XLA Modules:
  0.0 105.7 jit_solution(13423882823185361171)
XLA Ops:
  0.6 100.5 %moe_layer.1 = (bf16[2,8,32,768]{3,2,1,0:T(8,128)(2,1)S(1)}, bf16[256,512]{1,0:T(8,128)(2,1)S(1)}, bf16[4096,512]{1,0:T(8,128)(2,1)S(1)}, bf16[512,4096]{1,0:T(8,128)(2,1)S(1)}) custom-call(bf16[256,4096]{1,0:T(8,128)(2,1)} %tokens.1, bf16[256,4096]{1,0:T(8,128)(2,1)} %upstream.1, bf16[1,4096,512]{2,1,0:T(8,128)(2,1)} %w_in.1, bf16[1,512,4096]{2,1,0:T(8,128)(2,1)} %w_out.1, ...), custom_call_target="tpu_custom_call" | custom-call | flops 8000000000 | bytes 20000000 | tf_op jit(solution)/shard_map/moe_layer/pallas_call | solution.py:684
  101.1 4.4 %write_out.1 = (bf16[3072,128]{1,0:T(8,128)(2,1)}, bf16[256,512]{1,0:T(8,128)(2,1)}, bf16[1,4096,512]{2,1,0:T(8,128)(2,1)}, bf16[1,512,4096]{2,1,0:T(8,128)(2,1)}) custom-call(bf16[4096,512]{1,0:T(8,128)(2,1)S(1)} %get-tuple-element.12.grad_in_v, bf16[512,4096]{1,0:T(8,128)(2,1)S(1)} %get-tuple-element.13.grad_out_v, bf16[512,768]{1,0:T(8,128)(2,1)S(1)} %bitcast.9, ...), custom_call_target="tpu_custom_call" | custom-call | flops 200000000 | bytes 18000000 | tf_op jit(solution)/shard_map/write_out/pallas_call | solution.py:745

commit v6 on v5

--- a/solution.py
+++ b/solution.py
@@ -447,16 +447,13 @@
     lay_s[...] = layer.reshape(lay_s.shape)
     line_base = w.take(parts)
 
-    def to_line(i, carry):
-        to = lax.rem(t + i, parts)
-        w.send(line_base + i, lay_s.at[to], lay.at[z, y, t], (s, to), keep=False)
-        return carry
-
     def line_end(i, carry):
         w.copy(line_base + i, lay_s.at[0], lay_s.at[0], to_sib).wait_send()
         return carry
 
-    lax.fori_loop(1, parts, to_line, 0)
+    for to in (sib, far, far + other, left, left + other, right, right + other):
+        slot = line_base + lax.rem(to - t + parts, parts)
+        w.send(slot, lay_s.at[to], lay.at[z, y, t], (s, to), keep=False)
     lay[z, y, t] = lay_s[t]
 
     def from_chip(chip):
@@ -577,7 +574,6 @@
     for gather in qkv_rows[1:]:
         gather.near()
         gather.last()
-    back_b = send_back(1, reduce_b.result())
     for gather in qkv_rows:
         gather.sib_own()
         gather.sib_near()
@@ -598,6 +594,7 @@
     for zz in (z_plus, z_minus, z):
         for yy in (y_plus, y_minus):
             deliver(zz, yy)
+    back_b = send_back(1, reduce_b.result())
     for k in range(RING):
         second_p[k].last(0)
         second_p[k].last(1)
@@ -649,7 +646,7 @@
 
 
 def write_kernel(
-    grad_in_v, grad_out_v, products, grads, projected, grad_tokens, grad_in, grad_out, sems
+    grad_in_v, grad_out_v, products, grads, projected, grad_tokens, grad_in, grad_out, turned, sems
 ):
     copies = []
     for src, dst in ((grad_in_v, grad_in.at[0]), (grad_out_v, grad_out.at[0]), (grads, grad_tokens)):
@@ -662,7 +659,9 @@
         stacked = jnp.concatenate(
             [block[:, k * 128:(k + 1) * 128] for k in range(blocks)], axis=0
         )
-        projected[f * blocks:(f + BAND) * blocks, :] = dot(turn, stacked).astype(BF)
+        turned[f * blocks:(f + BAND) * blocks, :] = dot(turn, stacked).astype(BF)
+    copies.append(pltpu.make_async_copy(turned, projected, sems.at[len(copies)]))
+    copies[-1].start()
     for copy in copies:
         copy.wait()
 
@@ -751,8 +750,11 @@
             jax.ShapeDtypeStruct(w_out.shape, BF),
         ),
         in_specs=[vmem] * 4,
-        out_specs=(vmem, anywhere, anywhere, anywhere),
-        scratch_shapes=[pltpu.SemaphoreType.DMA((3,))],
+        out_specs=(anywhere, anywhere, anywhere, anywhere),
+        scratch_shapes=[
+            pltpu.VMEM((2 * n_tok * kinds * heads, lanes), BF),
+            pltpu.SemaphoreType.DMA((4,)),
+        ],
         compiler_params=pltpu.CompilerParams(vmem_limit_bytes=16 * 1024 * 1024),
         cost_estimate=pl.CostEstimate(
             flops=2 * 10**8, bytes_accessed=18 * 10**6, transcendentals=0

time: 106 us -> 106 us (level)
  no operation moved by 1% of the time
where the time goes in v6:
time: 106 us; the launch traced here: 105 us
  Pallas kernels  105 us (99%)
    pallas_call x1, Pallas kernels, on_device(): pl.pallas_call(layer_kernel, out_shape=(pltpu.VMEM((2, parts, n_tok // pa...  101 us
    pallas_call x1, Pallas kernels, on_device(): pl.pallas_call(write_kernel, out_shape=(jax.ShapeDtypeStruct((2 * n_tok *...  3.64 us

profile of v6, /device:TPU:5, one launch (start us, length us, event | category | flops | bytes accessed | tf_op | source)
XLA Modules:
  0.0 105.4 jit_solution(1724431128336062272)
XLA Ops:
  0.6 101.0 %moe_layer.1 = (bf16[2,8,32,768]{3,2,1,0:T(8,128)(2,1)S(1)}, bf16[256,512]{1,0:T(8,128)(2,1)S(1)}, bf16[4096,512]{1,0:T(8,128)(2,1)S(1)}, bf16[512,4096]{1,0:T(8,128)(2,1)S(1)}) custom-call(bf16[256,4096]{1,0:T(8,128)(2,1)} %tokens.1, bf16[256,4096]{1,0:T(8,128)(2,1)} %upstream.1, bf16[1,4096,512]{2,1,0:T(8,128)(2,1)} %w_in.1, bf16[1,512,4096]{2,1,0:T(8,128)(2,1)} %w_out.1, ...), custom_call_target="tpu_custom_call" | custom-call | flops 8000000000 | bytes 20000000 | tf_op jit(solution)/shard_map/moe_layer/pallas_call | solution.py:683
  101.6 3.6 %write_out.1 = (bf16[3072,128]{1,0:T(8,128)(2,1)}, bf16[256,512]{1,0:T(8,128)(2,1)}, bf16[1,4096,512]{2,1,0:T(8,128)(2,1)}, bf16[1,512,4096]{2,1,0:T(8,128)(2,1)}) custom-call(bf16[4096,512]{1,0:T(8,128)(2,1)S(1)} %get-tuple-element.12.grad_in_v, bf16[512,4096]{1,0:T(8,128)(2,1)S(1)} %get-tuple-element.13.grad_out_v, bf16[512,768]{1,0:T(8,128)(2,1)S(1)} %bitcast.9, ...), custom_call_target="tpu_custom_call" | custom-call | flops 200000000 | bytes 18000000 | tf_op jit(solution)/shard_map/write_out/pallas_call | solution.py:744
